TPU v7x, 32 devices: a whole 2x2x4 slice. The times are simulated.
32 devices in a mesh: dp: 4 (over y, core), blk: 8 (over z, x).
Axes of the slice: x: 2, y: 2, z: 4, core: 2. Of those that a mesh axis runs over, the one named last changes fastest.
Arguments:
- features: float32 [4, 16384, 128], P('dp', 'blk'), may hold values from -14 to 14
- func_points: float32 [4, 3, 4096, 128], P('dp', None, 'blk'), may hold values from -14 to 14
- coords: float32 [4, 2, 16384], P('dp', None, 'blk'), may hold values from -1 to 1
- presence: int32 [4, 3], P('dp'), may hold values from 0 to 1, as said below
- valid_rows: int32 [4, 3, 8], P('dp'), may hold values from 1 to 512, as said below
- norm_gain: float32 [2, 3, 128], replicated, may hold values from 0.25 to 1.75
- in_proj: float32 [2, 2, 3, 128, 128], replicated, may hold values from -1 to 1
- out_proj: float32 [2, 2, 128, 128], replicated, may hold values from -1.5 to 1.5
- router: float32 [2, 2, 4], replicated, may hold values from -4 to 4
- expert_up: float32 [2, 4, 128, 256], replicated, may hold values from -0.5 to 0.5
- expert_down: float32 [2, 4, 256, 128], replicated, may hold values from -0.375 to 0.375
- cotangent: float32 [4, 16384, 128], P('dp', 'blk'), may hold values from -6 to 6
Outputs:
- layer_output: float32 [4, 16384, 128], P('dp', 'blk')
- features_grad: float32 [4, 16384, 128], P('dp', 'blk')
- gain_grad: float32 [2, 3, 128], replicated
- in_proj_grad: float32 [2, 2, 3, 128, 128], replicated
- out_proj_grad: float32 [2, 2, 128, 128], replicated
- router_grad: float32 [2, 2, 4], replicated
- up_grad: float32 [2, 4, 128, 256], replicated
- down_grad: float32 [2, 4, 256, 128], replicated
Inputs may be any that keep to these rules, and one draw needn't show every extreme that they name: `presence`: every mesh has one function or more. `valid_rows`: the valid points of a block are its first slots; every block has one or more; each function of each mesh has a block of 512 valid points.
All inputs are finite; a program needn't handle non-finite values.
Results may differ from a plain program's by a relative error of at most 0.0003.
Values sent between devices are 32-bit elements; how exact they have to be, the bound alone decides.
A program may use at most 192 MiB of HBM per device.

v0:
```python
import jax
import jax.numpy as jnp
from jax import lax
from jax.sharding import PartitionSpec as P

HEADS = 8
HEAD_DIM = 16


PRECISE = lax.Precision.HIGHEST
eps = 1e-05


def carried_in(value, axis, join, neutral, backward):
    count, mine = (lax.axis_size(axis), lax.axis_index(axis))
    pieces = jax.tree.map(lambda part: lax.all_gather(part, axis), value)
    if backward:
        pieces = jax.tree.map(lambda part: part[::-1], pieces)
        mine = count - 1 - mine
    total = jax.tree.map(
        lambda part, zero: jnp.full_like(part, 0) + jnp.asarray(zero, part.dtype), value, neutral
    )

    def turn(position, total):
        longer = join(total, jax.tree.map(lambda part: part[position], pieces))
        return jax.tree.map(lambda new, old: jnp.where(position < mine, new, old), longer, total)

    return lax.fori_loop(0, count - 1, turn, total)


def spread(array, axis, root):
    mine = lax.axis_index(axis) == root
    return lax.psum(jnp.where(mine, array, jnp.zeros_like(array)), axis)


def layer_norm(stream, gain_row):
    row_mean = jnp.mean(stream, axis=-1, keepdims=True)
    centred = stream - row_mean
    row_var = jnp.mean(centred * centred, axis=-1, keepdims=True)
    return centred * lax.rsqrt(row_var + eps) * gain_row


def split_heads(matrix):
    return matrix.reshape(matrix.shape[:-1] + (HEADS, HEAD_DIM))


def head_softmax(matrix):
    return jax.nn.softmax(split_heads(matrix), axis=-1)


def linear(matrix, weight):
    return jnp.dot(matrix, weight, precision=PRECISE)


def pair_sum(earlier, later):
    return (earlier[0] + later[0], earlier[1] + later[1])


def forward_totals(summary, normalizer):
    before = carried_in(
        (summary, normalizer),
        "blk",
        pair_sum,
        (jnp.zeros_like(summary), jnp.zeros_like(normalizer)),
        False,
    )
    through = (before[0] + summary, before[1] + normalizer)
    return (
        spread(through[0], "blk", lax.axis_size("blk") - 1),
        spread(through[1], "blk", lax.axis_size("blk") - 1),
    )


def backward_totals(summary, normalizer):
    after = carried_in(
        (summary, normalizer),
        "blk",
        pair_sum,
        (jnp.zeros_like(summary), jnp.zeros_like(normalizer)),
        True,
    )
    through = (after[0] + summary, after[1] + normalizer)
    return (spread(through[0], "blk", 0), spread(through[1], "blk", 0))


def cross_inputs(stream, func_points, keep, gain_row, w_query, w_key, w_value):
    normed = layer_norm(stream, gain_row)
    queries = head_softmax(linear(normed, w_query))
    key_soft = head_softmax(linear(func_points, w_key)) * keep[..., None, None]
    values = split_heads(linear(func_points, w_value))
    summary = jnp.einsum("mfpha,mfphc->mfhac", key_soft, values, precision=PRECISE)
    normalizer = jnp.sum(key_soft, axis=2)
    return (queries, summary, normalizer)


def cross_then_self(
    stream, queries, summary, normalizer, presence_w, w_out, gain_row, w_query, w_key, w_value
):
    numerator = jnp.einsum("mnha,mfhac->mfnhc", queries, summary, precision=PRECISE)
    denominator = jnp.einsum("mnha,mfha->mfnh", queries, normalizer, precision=PRECISE)
    mixed = (
        jnp.einsum(
            "mf,mfnhc->mnhc", presence_w, numerator / denominator[..., None], precision=PRECISE
        )
        + queries
    )
    stream = stream + linear(mixed.reshape(stream.shape), w_out)
    normed = layer_norm(stream, gain_row)
    self_queries = head_softmax(linear(normed, w_query))
    key_soft = head_softmax(linear(normed, w_key))
    values = split_heads(linear(normed, w_value))
    self_summary = jnp.einsum("mnha,mnhc->mhac", key_soft, values, precision=PRECISE)
    self_normalizer = jnp.sum(key_soft, axis=1)
    return (stream, self_queries, self_summary, self_normalizer)


def self_then_experts(
    stream, queries, summary, normalizer, coords, w_out, gain_row, route_row, w_up, w_down
):
    numerator = jnp.einsum("mnha,mhac->mnhc", queries, summary, precision=PRECISE)
    denominator = jnp.einsum("mnha,mha->mnh", queries, normalizer, precision=PRECISE)
    mixed = numerator / denominator[..., None] + queries
    stream = stream + linear(mixed.reshape(stream.shape), w_out)
    normed = layer_norm(stream, gain_row)
    gate_probs = jax.nn.softmax(
        jnp.einsum("mcn,ce->mne", coords, route_row, precision=PRECISE), axis=-1
    )
    hidden = jax.nn.gelu(
        jnp.einsum("mnd,edh->mneh", normed, w_up, precision=PRECISE), approximate=True
    )
    return stream + jnp.einsum(
        "mneh,ehd->mnd", hidden * gate_probs[..., None], w_down, precision=PRECISE
    )


def on_device(
    features,
    func_points,
    coords,
    presence,
    valid_rows,
    norm_gain,
    in_proj,
    out_proj,
    router,
    expert_up,
    expert_down,
    cotangent,
):
    slot_count = func_points.shape[2]
    own_valid = lax.dynamic_slice_in_dim(valid_rows, lax.axis_index("blk"), 1, 2)
    keep = (jnp.arange(slot_count, dtype=jnp.int32)[None, None, :] < own_valid).astype(jnp.float32)
    presence_f = presence.astype(jnp.float32)
    presence_w = presence_f / jnp.sum(presence_f, axis=1, keepdims=True)
    layer_count = norm_gain.shape[0]
    stream = features
    pullers = []
    for layer_at in range(layer_count):

        def first_part(stream_in, gain_row, w_query, w_key, w_value):
            return cross_inputs(stream_in, func_points, keep, gain_row, w_query, w_key, w_value)

        def second_part(
            stream_in, queries, summary, normalizer, w_out, gain_row, w_query, w_key, w_value
        ):
            return cross_then_self(
                stream_in,
                queries,
                summary,
                normalizer,
                presence_w,
                w_out,
                gain_row,
                w_query,
                w_key,
                w_value,
            )

        def third_part(
            stream_in, queries, summary, normalizer, w_out, gain_row, route_row, w_up, w_down
        ):
            return self_then_experts(
                stream_in,
                queries,
                summary,
                normalizer,
                coords,
                w_out,
                gain_row,
                route_row,
                w_up,
                w_down,
            )

        (queries, summary, normalizer), pull_first = jax.vjp(
            first_part,
            stream,
            norm_gain[layer_at, 0],
            in_proj[layer_at, 0, 0],
            in_proj[layer_at, 0, 1],
            in_proj[layer_at, 0, 2],
        )
        summary, normalizer = forward_totals(summary, normalizer)
        (middle, self_queries, self_summary, self_normalizer), pull_second = jax.vjp(
            second_part,
            stream,
            queries,
            summary,
            normalizer,
            out_proj[layer_at, 0],
            norm_gain[layer_at, 1],
            in_proj[layer_at, 1, 0],
            in_proj[layer_at, 1, 1],
            in_proj[layer_at, 1, 2],
        )
        self_summary, self_normalizer = forward_totals(self_summary, self_normalizer)
        stream, pull_third = jax.vjp(
            third_part,
            middle,
            self_queries,
            self_summary,
            self_normalizer,
            out_proj[layer_at, 1],
            norm_gain[layer_at, 2],
            router[layer_at],
            expert_up[layer_at],
            expert_down[layer_at],
        )
        pullers.append((pull_first, pull_second, pull_third))
    grad_stream = cotangent
    layer_grads = [None] * layer_count
    for layer_at in reversed(range(layer_count)):
        pull_first, pull_second, pull_third = pullers[layer_at]
        (
            grad_mid,
            grad_squery,
            grad_ssum,
            grad_snorm,
            grad_wos,
            grad_gthree,
            grad_route,
            grad_up,
            grad_down,
        ) = pull_third(grad_stream)
        grad_ssum, grad_snorm = backward_totals(grad_ssum, grad_snorm)
        (
            grad_before,
            grad_query,
            grad_sum,
            grad_norm,
            grad_woc,
            grad_gtwo,
            grad_wqs,
            grad_wks,
            grad_wvs,
        ) = pull_second((grad_mid, grad_squery, grad_ssum, grad_snorm))
        grad_sum, grad_norm = backward_totals(grad_sum, grad_norm)
        grad_cross, grad_gone, grad_wqc, grad_wkc, grad_wvc = pull_first(
            (grad_query, grad_sum, grad_norm)
        )
        grad_stream = grad_before + grad_cross
        gain_part = jnp.stack([grad_gone, grad_gtwo, grad_gthree])
        inproj_part = jnp.stack(
            [jnp.stack([grad_wqc, grad_wkc, grad_wvc]), jnp.stack([grad_wqs, grad_wks, grad_wvs])]
        )
        outproj_part = jnp.stack([grad_woc, grad_wos])
        layer_grads[layer_at] = (
            gain_part,
            inproj_part,
            outproj_part,
            grad_route,
            grad_up,
            grad_down,
        )
    collected = [
        jnp.stack([layer_grads[layer_at][member] for layer_at in range(layer_count)])
        for member in range(6)
    ]
    gain_grad, in_proj_grad, out_proj_grad, router_grad, up_grad, down_grad = collected
    gain_grad, in_proj_grad, out_proj_grad, router_grad, up_grad, down_grad = lax.psum(
        (gain_grad, in_proj_grad, out_proj_grad, router_grad, up_grad, down_grad), ("dp", "blk")
    )
    return (
        stream,
        grad_stream,
        gain_grad,
        in_proj_grad,
        out_proj_grad,
        router_grad,
        up_grad,
        down_grad,
    )


def solution(mesh):
    placed = (
        P("dp", "blk", None),
        P("dp", None, "blk", None),
        P("dp", None, "blk"),
        P("dp", None),
        P("dp", None, None),
        P(),
        P(),
        P(),
        P(),
        P(),
        P(),
        P("dp", "blk", None),
    )
    return jax.shard_map(
        on_device,
        mesh=mesh,
        in_specs=placed,
        out_specs=(P("dp", "blk", None), P("dp", "blk", None), P(), P(), P(), P(), P(), P()),
        check_vma=False,
    )
```

profile of v0, /device:TPU:0, one launch (start us, length us, event | category | flops | bytes accessed | tf_op | source)
XLA Modules:
  0.0 1389.8 jit_solution(2260413398315035460)
XLA Ops:
  33.8 34.3 %all_gather.99 = f32[8,1,3,8,16]{4,3,2,1,0:T(8,128)} all-gather(f32[1,1,3,8,16]{4,3,2,1,0:T(8,128)S(1)} %all_gather.98), channel_id=1, replica_groups=mesh['dp'=4,'blk'=8] {'blk'}, dimensions={0}, use_global_device_ids=true | all-gather | bytes 13824 | tf_op jit(solution)/shard_map/all_gather | solution.py:16
  73.9 39.5 %all-gather = f32[24,8,16,16]{3,2,1,0:T(8,128)} all-gather(f32[3,8,16,16]{3,2,1,0:T(8,128)S(1)} %fusion.294), channel_id=2, replica_groups=mesh['dp'=4,'blk'=8] {'blk'}, dimensions={0}, use_global_device_ids=true | all-gather | bytes 221184 | tf_op jit(solution)/shard_map/all_gather | solution.py:16
  113.4 12.1 while.128
  127.9 38.6 %all-reduce.7 = (f32[3,8,16,16]{3,2,1,0:T(8,128)}, f32[3,8,16]{2,0,1:T(4,128)S(1)}) all-reduce(f32[3,8,16,16]{3,2,1,0:T(8,128)} %fusion.307, f32[3,8,16]{2,0,1:T(4,128)S(1)} %fusion.397), channel_id=1, replica_groups=mesh['dp'=4,'blk'=8] {'blk'}, use_global_device_ids=true, to_apply=%region_6.0 | all-reduce | flops 6528 | bytes 52224 | tf_op jit(solution)/shard_map/psum | solution.py:33
  169.4 3.7 fusion.107
  173.7 9.9 fusion.22
  186.5 3.8 bitcast_reduce_fusion.3
  199.9 32.7 %all_gather.107 = f32[8,1,3,8,16]{4,3,2,1,0:T(8,128)} all-gather(f32[1,1,3,8,16]{4,3,2,1,0:T(8,128)} %all_gather.106), channel_id=1, replica_groups=mesh['dp'=4,'blk'=8] {'blk'}, dimensions={0}, use_global_device_ids=true | all-gather | bytes 13824 | tf_op jit(solution)/shard_map/all_gather | solution.py:16
  235.6 35.7 %all-gather.2 = f32[24,8,16,16]{3,2,1,0:T(8,128)} all-gather(f32[3,8,16,16]{3,2,1,0:T(8,128)S(1)} %fusion.290), channel_id=4, replica_groups=mesh['dp'=4,'blk'=8] {'blk'}, dimensions={0}, use_global_device_ids=true | all-gather | bytes 221184 | tf_op jit(solution)/shard_map/all_gather | solution.py:16
  271.3 16.4 %while.130 = (s32[]{:T(128)}, f32[1,3,8,16,16]{4,3,2,1,0:T(8,128)S(1)}, f32[1,3,8,16]{3,2,1,0:T(8,128)}, s32[]{:T(128)}, f32[8,1,3,8,16,16]{5,4,3,2,1,0:T(8,128)...) while((s32[]{:T(128)}, f32[1,3,8,16,16]{4,3,2,1,0:T(8,128)S(1)}, ...), condition=%wide.region_31.32_spmd.clone, body=%wide.region_30.31_spmd.clone.sunk | while | flops 19588 | bytes 78459 | solution.py:28
  294.7 31.9 %all_gather.103 = f32[8,1,8,16]{3,2,1,0:T(8,128)} all-gather(f32[1,1,8,16]{3,2,1,0:T(8,128)} %all_gather.102), channel_id=1, replica_groups=mesh['dp'=4,'blk'=8] {'blk'}, dimensions={0}, use_global_device_ids=true | all-gather | bytes 4608 | tf_op jit(solution)/shard_map/all_gather | solution.py:16
  328.3 31.8 %all-gather.1 = f32[64,16,16]{2,1,0:T(8,128)S(1)} all-gather(f32[8,16,16]{2,1,0:T(8,128)S(1)} %fusion.272), channel_id=3, replica_groups=mesh['dp'=4,'blk'=8] {'blk'}, dimensions={0}, use_global_device_ids=true | all-gather | bytes 73728 | tf_op jit(solution)/shard_map/all_gather | solution.py:16
  360.2 5.1 while.129
  367.5 37.1 %all-reduce.6 = (f32[8,16,16]{2,1,0:T(8,128)S(1)}, f32[8,16]{1,0:T(8,128)S(1)}, f32[3,8,16,16]{3,2,1,0:T(8,128)S(1)}, f32[3,8,16]{2,0,1:T(4,128)S(1)}) all-reduce(f32[8,16,16]{2,1,0:T(8,128)S(1)} %fusion.347, f32[8,16]{1,0:T(8,128)S(1)} %select_bitcast_fusion.5, ...), channel_id=1, replica_groups=mesh['dp'=4,'blk'=8] {'blk'}, use_global_device_ids=true, to_apply=%region_19.20 | all-reduce | flops 8704 | bytes 69632 | tf_op jit(solution)/shard_map/psum | solution.py:33
  408.3 3.9 divide_add_fusion.1
  414.4 6.9 fusion.103
  421.4 7.8 fusion.443
  434.2 2.7 fusion.100
  437.5 10.0 fusion.20
  451.0 3.1 bitcast_reduce_fusion
  464.3 32.4 %all_gather.111 = f32[8,1,8,16]{3,2,1,0:T(8,128)} all-gather(f32[1,1,8,16]{3,2,1,0:T(8,128)} %all_gather.110), channel_id=1, replica_groups=mesh['dp'=4,'blk'=8] {'blk'}, dimensions={0}, use_global_device_ids=true | all-gather | bytes 4608 | tf_op jit(solution)/shard_map/all_gather | solution.py:16
  496.7 2.9 fusion.254
  500.3 33.4 %all-gather.3 = f32[64,16,16]{2,1,0:T(8,128)} all-gather(f32[8,16,16]{2,1,0:T(8,128)S(1)} %fusion.254), channel_id=5, replica_groups=mesh['dp'=4,'blk'=8] {'blk'}, dimensions={0}, use_global_device_ids=true | all-gather | bytes 73728 | tf_op jit(solution)/shard_map/all_gather | solution.py:16
  533.7 11.0 while.131
  546.8 36.1 %all-reduce.5 = (f32[8,16,16]{2,1,0:T(8,128)}, f32[8,16]{1,0:T(8,128)S(1)}) all-reduce(f32[8,16,16]{2,1,0:T(8,128)} %fusion.333, f32[8,16]{1,0:T(8,128)S(1)} %select_bitcast_fusion.4), channel_id=1, replica_groups=mesh['dp'=4,'blk'=8] {'blk'}, use_global_device_ids=true, to_apply=%region_45.46 | all-reduce | flops 2176 | bytes 17408 | tf_op jit(solution)/shard_map/psum | solution.py:33
  586.2 2.6 copy.194
  588.8 2.9 divide_add_fusion
  594.0 7.0 fusion.96
  601.1 9.8 fusion.79
  610.8 14.6 %multiply_reduce_fusion = (f32[2048,4]{0,1:T(4,128)}, f32[2048,4,256]{0,2,1:T(8,128)S(1)}) fusion(f32[2048,4,256]{0,2,1:T(8,128)S(1)} %fusion.96, f32[2048,4]{0,1:T(4,128)S(1)} %broadcast_divide_fusion, f32[2,4,256,128]{3,2,1,0:T(8,128)S(1)} %copy-done.218, f32[1,2048,128]{2,1,0:T(8,128)S(1)} %copy-done.84), kind=kOutput, calls=%fused_computation.32 | convolution fusion | flops 3269451776 | bytes 18415616 | tf_op jit(solution)/shard_map/transpose(jvp(mneh,ehd->mnd))/dot_general | solution.py:131
  625.4 7.5 convolution_bitcast_fusion.16
  632.9 4.8 fusion.132
  647.3 30.4 %all-gather.5 = f32[64,16]{1,0:T(8,128)S(1)} all-gather(f32[8,16]{1,0:T(8,128)S(1)} %bitcast.1387), channel_id=7, replica_groups=mesh['dp'=4,'blk'=8] {'blk'}, dimensions={0}, use_global_device_ids=true | all-gather | bytes 4608 | tf_op jit(solution)/shard_map/all_gather | solution.py:16
  678.3 31.3 %all-gather.4 = f32[8,8,16,16]{3,2,1,0:T(8,128)S(1)} all-gather(f32[1,8,16,16]{3,2,1,0:T(8,128)S(1)} %convolution_bitcast_fusion.35), channel_id=6, replica_groups=mesh['dp'=4,'blk'=8] {'blk'}, dimensions={0}, use_global_device_ids=true | all-gather | bytes 73728 | tf_op jit(solution)/shard_map/all_gather | solution.py:16
  710.5 10.9 while.132
  722.1 35.0 %all-reduce.4 = (f32[8,16,16]{2,1,0:T(8,128)S(1)}, f32[8,16]{1,0:T(8,128)S(1)}) all-reduce(f32[8,16,16]{2,1,0:T(8,128)} %select_bitcast_fusion.3, f32[8,16]{1,0:T(8,128)S(1)} %fusion.412), channel_id=1, replica_groups=mesh['dp'=4,'blk'=8] {'blk'}, use_global_device_ids=true, to_apply=%region_58.59 | all-reduce | flops 2176 | bytes 17408 | tf_op jit(solution)/shard_map/psum | solution.py:33
  763.2 3.4 multiply_reduce_fusion.7
  794.7 9.7 fusion.76
  804.5 14.2 %multiply_reduce_fusion.1 = (f32[2048,4]{0,1:T(4,128)}, f32[2048,4,256]{0,2,1:T(8,128)S(1)}) fusion(f32[2048,4,256]{0,2,1:T(8,128)S(1)} %bitcast.1328, f32[2048,4]{0,1:T(4,128)S(1)} %copy-done.191, f32[2,4,256,128]{3,2,1,0:T(8,128)S(1)} %copy-done.219, f32[1,2048,128]{1,2,0:T(8,128)S(1)} %add_add_fusion.9), kind=kOutput, calls=%fused_computation.33 | convolution fusion | flops 3269451776 | bytes 18415616 | tf_op jit(solution)/shard_map/transpose(jvp(mneh,ehd->mnd))/dot_general | solution.py:131
  818.7 8.0 convolution_bitcast_fusion.17
  826.7 4.8 fusion.123
  841.9 31.9 %all-gather.7 = f32[64,16]{1,0:T(8,128)} all-gather(f32[8,16]{1,0:T(8,128)S(1)} %bitcast.1389), channel_id=9, replica_groups=mesh['dp'=4,'blk'=8] {'blk'}, dimensions={0}, use_global_device_ids=true | all-gather | bytes 4608 | tf_op jit(solution)/shard_map/all_gather | solution.py:16
  875.2 31.4 %all-gather.6 = f32[8,8,16,16]{3,2,1,0:T(8,128)S(1)} all-gather(f32[1,8,16,16]{3,2,1,0:T(8,128)} %convolution_bitcast_fusion.34), channel_id=8, replica_groups=mesh['dp'=4,'blk'=8] {'blk'}, dimensions={0}, use_global_device_ids=true | all-gather | bytes 73728 | tf_op jit(solution)/shard_map/all_gather | solution.py:16
  907.4 15.2 %while.133 = (s32[]{:T(128)}, f32[1,8,16,16]{3,2,1,0:T(8,128)S(1)}, f32[1,8,16]{2,1,0:T(8,128)}, s32[]{:T(128)}, f32[8,1,8,16,16]{4,3,2,1,0:T(8,128)}, /*index=5*/f32[8,1,8,16]{3,2,1,0:T(8,128)}, s32[]{:T(128)}, s32[]{:T(128)}) while((s32[]{:T(128)}, f32[1,8,16,16]{3,2,1,0:T(8,128)S(1)}, f32[1,8,16]{2,1,0:T(8,128)}, s32[]{:T(128)}, ...), condition=%wide.region_72.73_spmd.clone, body=%wide.region_71.72_spmd.clone.sunk | while | flops 6532 | bytes 26235 | solution.py:28
  925.4 36.3 %all-reduce.3 = (f32[8,16,16]{2,1,0:T(8,128)}, f32[8,16]{1,0:T(8,128)}) all-reduce(f32[8,16,16]{2,1,0:T(8,128)} %select_bitcast_fusion.2, f32[8,16]{1,0:T(8,128)} %fusion.410), channel_id=1, replica_groups=mesh['dp'=4,'blk'=8] {'blk'}, use_global_device_ids=true, to_apply=%region_73.74 | all-reduce | flops 2176 | bytes 17408 | tf_op jit(solution)/shard_map/psum | solution.py:33
  963.8 2.5 convolution_bitcast_fusion.30
  968.2 3.4 multiply_reduce_fusion.3
  990.9 30.7 %all-gather.11 = f32[8,3,8,16]{3,2,1,0:T(8,128)S(1)} all-gather(f32[1,3,8,16]{3,2,1,0:T(8,128)S(1)} %copy.221), channel_id=13, replica_groups=mesh['dp'=4,'blk'=8] {'blk'}, dimensions={0}, use_global_device_ids=true | all-gather | bytes 13824 | tf_op jit(solution)/shard_map/all_gather | solution.py:16
  1022.2 30.5 %all-gather.9 = f32[8,3,8,16]{3,2,1,0:T(8,128)S(1)} all-gather(f32[1,3,8,16]{3,2,1,0:T(8,128)S(1)} %copy.212), channel_id=11, replica_groups=mesh['dp'=4,'blk'=8] {'blk'}, dimensions={0}, use_global_device_ids=true | all-gather | bytes 13824 | tf_op jit(solution)/shard_map/all_gather | solution.py:16
  1058.2 9.2 fusion.85
  1067.4 9.4 fusion.82
  1076.8 33.6 %all-gather.8 = f32[8,3,8,16,16]{4,3,2,1,0:T(8,128)S(1)} all-gather(f32[1,3,8,16,16]{4,3,2,1,0:T(8,128)S(1)} %fusion.82), channel_id=10, replica_groups=mesh['dp'=4,'blk'=8] {'blk'}, dimensions={0}, use_global_device_ids=true | all-gather | bytes 221184 | tf_op jit(solution)/shard_map/all_gather | solution.py:16
  1111.7 7.3 while.134
  1120.3 33.5 %all-gather.10 = f32[8,3,8,16,16]{4,3,2,1,0:T(8,128)S(1)} all-gather(f32[1,3,8,16,16]{4,3,2,1,0:T(8,128)S(1)} %fusion.85), channel_id=12, replica_groups=mesh['dp'=4,'blk'=8] {'blk'}, dimensions={0}, use_global_device_ids=true | all-gather | bytes 221184 | tf_op jit(solution)/shard_map/all_gather | solution.py:16
  1155.1 21.4 %while.135 = (s32[]{:T(128)}, f32[1,3,8,16,16]{4,3,2,1,0:T(8,128)}, f32[1,3,8,16]{3,2,1,0:T(8,128)}, s32[]{:T(128)}, f32[8,1,3,8,16,16]{5,4,3,2,1,0:T(8,128)}, /...) while((s32[]{:T(128)}, f32[1,3,8,16,16]{4,3,2,1,0:T(8,128)}, f32[1,3,8,16]{3,2,1,0:T(8,128)}, ...), condition=%wide.region_96.97_spmd.clone, body=%wide.region_95.96_spmd.clone.sunk | while | flops 19588 | bytes 78459 | solution.py:28
  1179.6 38.6 %all-reduce.2 = (f32[3,8,16,16]{3,2,1,0:T(8,128)}, f32[3,8,16]{2,0,1:T(4,128)}, f32[3,8,16,16]{3,2,1,0:T(8,128)}, f32[3,8,16]{2,0,1:T(4,128)}) all-reduce(f32[3,8,16,16]{3,2,1,0:T(8,128)} %select_bitcast_fusion, f32[3,8,16]{2,0,1:T(4,128)} %fusion.391, ...), channel_id=1, replica_groups=mesh['dp'=4,'blk'=8] {'blk'}, use_global_device_ids=true, to_apply=%region_98.99 | all-reduce | flops 13056 | bytes 104448 | tf_op jit(solution)/shard_map/psum | solution.py:33
  1236.8 11.2 fusion.52
  1248.0 3.1 fusion.115
  1251.7 2.6 copy.232
  1256.4 37.6 %all-reduce = (f32[2,3,128]{2,1,0:T(4,128)S(1)}, f32[2,2,4]{2,1,0:T(2,128)}) all-reduce(f32[2,3,128]{2,1,0:T(4,128)S(1)} %pad_maximum_fusion.4, f32[2,2,4]{2,1,0:T(2,128)S(1)} %pad_maximum_fusion.5), channel_id=1, replica_groups=mesh['dp'=4,'blk'=8] {'dp','blk'}, use_global_device_ids=true, to_apply=%region_89.90 | all-reduce | flops 784 | bytes 6272 | tf_op jit(solution)/shard_map/psum | solution.py:280
  1294.6 2.5 add_add_fusion.6
  1297.2 2.5 copy.233
  1299.7 74.5 %all-reduce.10.cloned.1.call-done = (f32[2,2,3,128,128]{4,3,2,1,0:T(8,128)}, f32[2,2,128,128]{3,2,1,0:T(8,128)}, f32[2,4,128,256]{2,3,1,0:T(8,128)}, f32[2,4,256,128]{3,2,1,0:T(8,128)}) async-done(((f32[2,2,3,128,128]{4,3,2,1,0:T(8,128)}, f32[2,2,128,128]{3,2,1,0:T(8,128)}, f32[2,4,128,256]{2,3,1,0:T(8,128)}, f32[2,4,256,128]{3,2,1,0:T(8,128)}), (f32[2,2,3,128,128]{4,3,2,1,0:T(8,128)}, ...) | async-done | bytes 3145744 | tf_op jit(solution)/shard_map/psum | solution.py:280
  1374.2 2.5 copy.235
  (820 shorter events, 318.5 us)
Async XLA Ops:
  7.2 1367.1 %all-reduce.10.cloned.1.call-start = ((), (), s32[]{:S(2)}) async-start(), calls=%async_computation | async-start | bytes 6291456 | tf_op jit(solution)/shard_map/psum | solution.py:280
  15.2 54.3 %copy-start.75 = (f32[3,512,8]{1,2,0:T(8,128)}, f32[3,512,8]{1,2,0:T(8,128)S(1)}, u32[]{:S(2)}) copy-start(f32[3,512,8]{1,2,0:T(8,128)S(1)} %get-tuple-element.1396) | copy-start | bytes 147460
  17.0 52.4 %copy-start.22 = (f32[3,512,128]{1,2,0:T(8,128)}, f32[3,512,128]{1,2,0:T(8,128)S(1)}, u32[]{:S(2)}) copy-start(f32[3,512,128]{1,2,0:T(8,128)S(1)} %get-tuple-element.1395) | copy-start | bytes 2359300
  17.0 52.4 %copy-start.73 = (f32[3,512,8]{1,2,0:T(8,128)}, f32[3,512,8]{1,2,0:T(8,128)S(1)}, u32[]{:S(2)}) copy-start(f32[3,512,8]{1,2,0:T(8,128)S(1)} %get-tuple-element.1394) | copy-start | bytes 147460
  18.1 51.4 %copy-start.152 = (f32[3,512]{1,0:T(4,128)}, f32[3,512]{1,0:T(4,128)S(1)}, u32[]{:S(2)}) copy-start(f32[3,512]{1,0:T(4,128)S(1)} %fusion.402) | copy-start | bytes 18436
  18.6 50.9 %copy-start.90 = (f32[3,512,8]{1,2,0:T(8,128)}, f32[3,512,8]{1,2,0:T(8,128)S(1)}, u32[]{:S(2)}) copy-start(f32[3,512,8]{1,2,0:T(8,128)S(1)} %get-tuple-element.1462) | copy-start | bytes 147460
  18.6 50.9 %copy-start.92 = (f32[3,512,8]{1,2,0:T(8,128)}, f32[3,512,8]{1,2,0:T(8,128)S(1)}, u32[]{:S(2)}) copy-start(f32[3,512,8]{1,2,0:T(8,128)S(1)} %get-tuple-element.1463) | copy-start | bytes 147460
  26.9 163.3 %copy-start.182 = (f32[128]{0:T(128)}, f32[128]{0:T(128)S(1)}, u32[]{:S(2)}) copy-start(f32[128]{0:T(128)S(1)} %get-tuple-element.1389) | copy-start | bytes 1540
  28.5 155.7 %copy-start.1 = (f32[1,2048,128]{1,2,0:T(8,128)}, f32[1,2048,128]{1,2,0:T(8,128)S(1)}, u32[]{:S(2)}) copy-start(f32[1,2048,128]{1,2,0:T(8,128)S(1)} %copy.169) | copy-start | bytes 3145732
  30.5 39.0 %copy-start.106 = (f32[2048]{0:T(1024)}, f32[2048]{0:T(1024)S(1)}, u32[]{:S(2)}) copy-start(f32[2048]{0:T(1024)S(1)} %broadcast_multiply_fusion.5) | copy-start | bytes 24580
  33.8 36.2 %copy-start.60 = (f32[3,512,8,16]{1,3,2,0:T(8,128)}, f32[3,512,8,16]{1,3,2,0:T(8,128)S(1)}, u32[]{:S(2)}) copy-start(f32[3,512,8,16]{1,3,2,0:T(8,128)S(1)} %fusion.202) | copy-start | bytes 2359300
  72.2 111.4 %copy-start.13 = (f32[2048,128]{0,1:T(8,128)}, f32[2048,128]{0,1:T(8,128)S(1)}, u32[]{:S(2)}) copy-start(f32[2048,128]{0,1:T(8,128)S(1)} %get-tuple-element.1399) | copy-start | bytes 3145732
  72.2 111.4 %copy-start.66 = (f32[2048,8]{0,1:T(8,128)}, f32[2048,8]{0,1:T(8,128)S(1)}, u32[]{:S(2)}) copy-start(f32[2048,8]{0,1:T(8,128)S(1)} %get-tuple-element.1398) | copy-start | bytes 196612
  183.6 49.0 %copy-start.76 = (f32[3,512,8]{1,2,0:T(8,128)S(1)}, f32[3,512,8]{1,2,0:T(8,128)}, u32[]{:S(2)}) copy-start(f32[3,512,8]{1,2,0:T(8,128)} %copy-done.75) | copy-start | bytes 147460
  183.7 49.0 %copy-start.153 = (f32[3,512]{1,0:T(4,128)S(1)}, f32[3,512]{1,0:T(4,128)}, u32[]{:S(2)}) copy-start(f32[3,512]{1,0:T(4,128)} %copy-done.152) | copy-start | bytes 18436
  184.2 48.4 %copy-start.93 = (f32[3,512,8]{1,2,0:T(8,128)S(1)}, f32[3,512,8]{1,2,0:T(8,128)}, u32[]{:S(2)}) copy-start(f32[3,512,8]{1,2,0:T(8,128)} %copy-done.92) | copy-start | bytes 147460
  186.3 103.1 %copy-start.86 = (f32[2048]{0:T(1024)}, f32[2048]{0:T(1024)S(1)}, u32[]{:S(2)}) copy-start(f32[2048]{0:T(1024)S(1)} %broadcast_multiply_fusion.4) | copy-start | bytes 24580
  186.5 46.1 %copy-start.157 = (f32[2048]{0:T(1024)}, f32[2048]{0:T(1024)S(1)}, u32[]{:S(2)}) copy-start(f32[2048]{0:T(1024)S(1)} %multiply_reduce_fusion.14) | copy-start | bytes 24580
  186.5 102.9 %copy-start.88 = (f32[2048]{0:T(1024)}, f32[2048]{0:T(1024)S(1)}, u32[]{:S(2)}) copy-start(f32[2048]{0:T(1024)S(1)} %fusion.404) | copy-start | bytes 24580
  192.4 134.2 %copy-start.18 = (f32[2048,128]{0,1:T(8,128)}, f32[2048,128]{0,1:T(8,128)S(1)}, u32[]{:S(2)}) copy-start(f32[2048,128]{0,1:T(8,128)S(1)} %get-tuple-element.1403) | copy-start | bytes 3145732
  192.4 134.1 %copy-start.71 = (f32[2048,8]{0,1:T(8,128)}, f32[2048,8]{0,1:T(8,128)S(1)}, u32[]{:S(2)}) copy-start(f32[2048,8]{0,1:T(8,128)S(1)} %get-tuple-element.1402) | copy-start | bytes 196612
  192.7 135.6 %copy-start.82 = (f32[2048,8]{0,1:T(8,128)}, f32[2048,8]{0,1:T(8,128)S(1)}, u32[]{:S(2)}) copy-start(f32[2048,8]{0,1:T(8,128)S(1)} %fusion.195) | copy-start | bytes 196612
  199.9 32.7 %copy-start.62 = (f32[3,512,8,16]{1,3,2,0:T(8,128)}, f32[3,512,8,16]{1,3,2,0:T(8,128)S(1)}, u32[]{:S(2)}) copy-start(f32[3,512,8,16]{1,3,2,0:T(8,128)S(1)} %fusion.200) | copy-start | bytes 2359300
  235.6 124.6 %copy-start.151 = (f32[1,8,16]{2,1,0:T(8,128)S(1)}, f32[1,8,16]{2,1,0:T(8,128)}, u32[]{:S(2)}) copy-start(f32[1,8,16]{2,1,0:T(8,128)} %custom-call.3) | copy-start | bytes 1540
  235.6 169.1 %copy-start.98 = (f32[2048,8]{0,1:T(8,128)S(1)}, f32[2048,8]{0,1:T(8,128)}, u32[]{:S(2)}) copy-start(f32[2048,8]{0,1:T(8,128)} %get-tuple-element.1404) | copy-start | bytes 196612
  287.7 78.4 %copy-start.105 = (f32[1,3,8,16]{3,2,1,0:T(8,128)S(1)}, f32[1,3,8,16]{3,2,1,0:T(8,128)}, u32[]{:S(2)}) copy-start(f32[1,3,8,16]{3,2,1,0:T(8,128)} %get-tuple-element.893) | copy-start | bytes 4612
  287.7 119.7 %copy-start.118 = (f32[2048,4]{0,1:T(4,128)S(1)}, f32[2048,4]{0,1:T(4,128)}, u32[]{:S(2)}) copy-start(f32[2048,4]{0,1:T(4,128)} %get-tuple-element.1409) | copy-start | bytes 98308
  287.7 119.7 %copy-start.169 = (f32[2048]{0:T(1024)S(1)}, f32[2048]{0:T(1024)}, u32[]{:S(2)}) copy-start(f32[2048]{0:T(1024)} %get-tuple-element.1408) | copy-start | bytes 24580
  287.7 119.7 %copy-start.171 = (f32[2048]{0:T(1024)S(1)}, f32[2048]{0:T(1024)}, u32[]{:S(2)}) copy-start(f32[2048]{0:T(1024)} %get-tuple-element.1424) | copy-start | bytes 24580
  289.4 78.1 %copy-start.97 = (f32[3,8,16,16]{3,2,1,0:T(8,128)S(1)}, f32[3,8,16,16]{3,2,1,0:T(8,128)}, u32[]{:S(2)}) copy-start(f32[3,8,16,16]{3,2,1,0:T(8,128)} %fusion.305) | copy-start | bytes 73732
  291.5 36.8 %copy-start.56 = (f32[2048,8,16]{0,2,1:T(8,128)}, f32[2048,8,16]{0,2,1:T(8,128)S(1)}, u32[]{:S(2)}) copy-start(f32[2048,8,16]{0,2,1:T(8,128)S(1)} %fusion.105) | copy-start | bytes 3145732
  328.3 31.9 %copy-start.125 = (f32[8,16,16]{2,1,0:T(8,128)}, f32[8,16,16]{2,1,0:T(8,128)S(1)}, u32[]{:S(2)}) copy-start(f32[8,16,16]{2,1,0:T(8,128)S(1)} %fusion.272) | copy-start | bytes 24580
  404.6 28.1 %copy-start.203 = (f32[3,8,16]{2,0,1:T(4,128)}, f32[3,8,16]{2,0,1:T(4,128)S(1)}, u32[]{:S(2)}) copy-start(f32[3,8,16]{2,0,1:T(4,128)S(1)} %get-tuple-element.1369) | copy-start | bytes 4612
  404.6 29.6 %copy-start.145 = (f32[3,8,16,16]{3,2,1,0:T(8,128)}, f32[3,8,16,16]{3,2,1,0:T(8,128)S(1)}, u32[]{:S(2)}) copy-start(f32[3,8,16,16]{3,2,1,0:T(8,128)S(1)} %get-tuple-element.1368) | copy-start | bytes 73732
  408.3 177.9 %copy-start.167 = (f32[2048]{0:T(1024)}, f32[2048]{0:T(1024)S(1)}, u32[]{:S(2)}) copy-start(f32[2048]{0:T(1024)S(1)} %get-tuple-element.1461) | copy-start | bytes 24580
  450.2 83.5 %copy-start.150 = (f32[1,8,16]{2,1,0:T(8,128)S(1)}, f32[1,8,16]{2,1,0:T(8,128)}, u32[]{:S(2)}) copy-start(f32[1,8,16]{2,1,0:T(8,128)} %custom-call.7) | copy-start | bytes 1540
  456.3 129.9 %copy-start.120 = (f32[2048,4]{0,1:T(4,128)S(1)}, f32[2048,4]{0,1:T(4,128)}, u32[]{:S(2)}) copy-start(f32[2048,4]{0,1:T(4,128)} %get-tuple-element.1425) | copy-start | bytes 98308
  456.3 129.9 %copy-start.172 = (f32[2048]{0:T(1024)S(1)}, f32[2048]{0:T(1024)}, u32[]{:S(2)}) copy-start(f32[2048]{0:T(1024)} %get-tuple-element.1424) | copy-start | bytes 24580
  461.7 35.0 %copy-start.58 = (f32[2048,8,16]{0,2,1:T(8,128)}, f32[2048,8,16]{0,2,1:T(8,128)S(1)}, u32[]{:S(2)}) copy-start(f32[2048,8,16]{0,2,1:T(8,128)S(1)} %fusion.98) | copy-start | bytes 3145732
  586.2 24.6 %copy-start.188 = (f32[2048,4]{0,1:T(4,128)}, f32[2048,4]{0,1:T(4,128)S(1)}, u32[]{:S(2)}) copy-start(f32[2048,4]{0,1:T(4,128)S(1)} %broadcast_divide_fusion) | copy-start | bytes 98308
  593.8 45.5 %copy-start.3 = (f32[1,2048,128]{1,2,0:T(8,128)}, f32[1,2048,128]{1,2,0:T(8,128)S(1)}, u32[]{:S(2)}) copy-start(f32[1,2048,128]{1,2,0:T(8,128)S(1)} %get-tuple-element.1427) | copy-start | bytes 3145732
  643.2 67.3 %copy-start.149 = (f32[1,8,16]{2,1,0:T(8,128)S(1)}, f32[1,8,16]{2,1,0:T(8,128)}, u32[]{:S(2)}) copy-start(f32[1,8,16]{2,1,0:T(8,128)} %custom-call.9) | copy-start | bytes 1540
  644.9 114.7 %copy-start.186 = (f32[128]{0:T(128)S(1)}, f32[128]{0:T(128)}, u32[]{:S(2)}) copy-start(f32[128]{0:T(128)} %get-tuple-element.1391) | copy-start | bytes 1540
  837.1 70.3 %copy-start.63 = (f32[1,8,16,16]{3,2,1,0:T(8,128)S(1)}, f32[1,8,16,16]{3,2,1,0:T(8,128)}, u32[]{:S(2)}) copy-start(f32[1,8,16,16]{3,2,1,0:T(8,128)} %custom-call.10) | copy-start | bytes 24580
  837.1 124.5 %copy-start.19 = (f32[2048,128]{0,1:T(8,128)S(1)}, f32[2048,128]{0,1:T(8,128)}, u32[]{:S(2)}) copy-start(f32[2048,128]{0,1:T(8,128)} %copy-done.18) | copy-start | bytes 3145732
  837.1 124.5 %copy-start.72 = (f32[2048,8]{0,1:T(8,128)S(1)}, f32[2048,8]{0,1:T(8,128)}, u32[]{:S(2)}) copy-start(f32[2048,8]{0,1:T(8,128)} %copy-done.71) | copy-start | bytes 196612
  837.1 124.5 %copy-start.83 = (f32[2048,8]{0,1:T(8,128)S(1)}, f32[2048,8]{0,1:T(8,128)}, u32[]{:S(2)}) copy-start(f32[2048,8]{0,1:T(8,128)} %copy-done.82) | copy-start | bytes 196612
  839.4 124.3 %copy-start.87 = (f32[2048]{0:T(1024)S(1)}, f32[2048]{0:T(1024)}, u32[]{:S(2)}) copy-start(f32[2048]{0:T(1024)} %copy-done.86) | copy-start | bytes 24580
  839.4 124.3 %copy-start.89 = (f32[2048]{0:T(1024)S(1)}, f32[2048]{0:T(1024)}, u32[]{:S(2)}) copy-start(f32[2048]{0:T(1024)} %copy-done.88) | copy-start | bytes 24580
  841.9 31.9 %copy-start.205 = (f32[8,1,16]{2,1,0:T(1,128)}, f32[8,1,16]{2,1,0:T(1,128)S(1)}, u32[]{:S(2)}) copy-start(f32[8,1,16]{2,1,0:T(1,128)S(1)} %fusion.314) | copy-start | bytes 1540
  924.1 47.5 %copy-start.101 = (f32[2048,8]{0,1:T(8,128)S(1)}, f32[2048,8]{0,1:T(8,128)}, u32[]{:S(2)}) copy-start(f32[2048,8]{0,1:T(8,128)} %copy-done.99) | copy-start | bytes 196612
  987.3 65.4 %copy-start.144 = (f32[3,8,16,16]{3,2,1,0:T(8,128)S(1)}, f32[3,8,16,16]{3,2,1,0:T(8,128)}, u32[]{:S(2)}) copy-start(f32[3,8,16,16]{3,2,1,0:T(8,128)} %get-tuple-element.1370) | copy-start | bytes 73732
  987.3 65.4 %copy-start.174 = (f32[2048,8]{0,1:T(8,128)S(1)}, f32[2048,8]{0,1:T(8,128)}, u32[]{:S(2)}) copy-start(f32[2048,8]{0,1:T(8,128)} %multiply_divide_fusion.2) | copy-start | bytes 196612
  1058.2 53.4 %copy-start.47 = (f32[1,3,8,16,16]{4,3,2,1,0:T(8,128)S(1)}, f32[1,3,8,16,16]{4,3,2,1,0:T(8,128)}, u32[]{:S(2)}) copy-start(f32[1,3,8,16,16]{4,3,2,1,0:T(8,128)} %custom-call.12) | copy-start | bytes 73732
  1058.2 53.4 %copy-start.104 = (f32[1,3,8,16]{3,2,1,0:T(8,128)S(1)}, f32[1,3,8,16]{3,2,1,0:T(8,128)}, u32[]{:S(2)}) copy-start(f32[1,3,8,16]{3,2,1,0:T(8,128)} %custom-call.13) | copy-start | bytes 4612
  1067.4 86.4 %copy-start.94 = (f32[1,3,8,16,16]{4,3,2,1,0:T(8,128)}, f32[1,3,8,16,16]{4,3,2,1,0:T(8,128)S(1)}, u32[]{:S(2)}) copy-start(f32[1,3,8,16,16]{4,3,2,1,0:T(8,128)S(1)} %fusion.85) | copy-start | bytes 73732
  1110.4 108.7 %copy-start.26 = (f32[3,512,128]{1,2,0:T(8,128)S(1)}, f32[3,512,128]{1,2,0:T(8,128)}, u32[]{:S(2)}) copy-start(f32[3,512,128]{1,2,0:T(8,128)} %copy-done.25) | copy-start | bytes 2359300
  1110.4 108.7 %copy-start.77 = (f32[3,512,8]{1,2,0:T(8,128)S(1)}, f32[3,512,8]{1,2,0:T(8,128)}, u32[]{:S(2)}) copy-start(f32[3,512,8]{1,2,0:T(8,128)} %copy-done.75) | copy-start | bytes 147460
  1155.1 72.2 %copy-start.23 = (f32[3,512,128]{1,2,0:T(8,128)S(1)}, f32[3,512,128]{1,2,0:T(8,128)}, u32[]{:S(2)}) copy-start(f32[3,512,128]{1,2,0:T(8,128)} %copy-done.22) | copy-start | bytes 2359300
  1155.1 72.2 %copy-start.74 = (f32[3,512,8]{1,2,0:T(8,128)S(1)}, f32[3,512,8]{1,2,0:T(8,128)}, u32[]{:S(2)}) copy-start(f32[3,512,8]{1,2,0:T(8,128)} %copy-done.73) | copy-start | bytes 147460
  1155.1 72.2 %copy-start.91 = (f32[3,512,8]{1,2,0:T(8,128)S(1)}, f32[3,512,8]{1,2,0:T(8,128)}, u32[]{:S(2)}) copy-start(f32[3,512,8]{1,2,0:T(8,128)} %copy-done.90) | copy-start | bytes 147460
  1236.8 19.6 %copy-start.215 = (f32[128]{0:T(128)S(1)}, f32[128]{0:T(128)}, u32[]{:S(2)}) copy-start(f32[128]{0:T(128)} %get-tuple-element.1244) | copy-start | bytes 1540
  1236.8 19.6 %copy-start.216 = (f32[128]{0:T(128)S(1)}, f32[128]{0:T(128)}, u32[]{:S(2)}) copy-start(f32[128]{0:T(128)} %get-tuple-element.1242) | copy-start | bytes 1540
  1248.0 46.7 %copy-start.30 = (f32[1,2048,128]{1,2,0:T(8,128)S(1)}, f32[1,2048,128]{1,2,0:T(8,128)}, u32[]{:S(2)}) copy-start(f32[1,2048,128]{1,2,0:T(8,128)} %copy-done.29) | copy-start | bytes 3145732
  (163 other events, 1365.9 us)
Sparse Core Ops, SparseCore 0:
  1236.7 137.5 all-reduce.9
where the time goes:
time: 1400 us; the launch traced here: 1390 us
  blocking collectives  784 us (56%)
  matrix products  300 us (21%)
  other arithmetic  162 us (12%)
  waiting for transfers between devices  74.5 us (5%)
  local copies, waits for them, and re-layouts  49 us (4%)
  between operations  18.3 us (1%)
    all_gather x16, blocking collectives, carried_in(): pieces = jax.tree.map(lambda part: lax.all_gather(part, axis), value)  525 us
    psum x6, blocking collectives, spread(): return lax.psum(jnp.where(mine, array, jnp.zeros_like(array)), axis)  222 us
    select_n x112, other arithmetic, turn(): jnp.where(position < mine, new, old)  98.2 us
    dot_general x44, matrix products, linear(): return jnp.dot(matrix, weight, precision=PRECISE)  83.5 us
    psum x1, waiting for transfers between devices, on_device(): lax.psum((gain_grad, in_proj_grad, out_proj_grad, router_grad, up_grad, d...  74.5 us
    dot_general x6, matrix products, self_then_experts(): jnp.einsum('mneh,ehd->mnd', hidden * gate_probs[..., None], w_down, preci...  67.2 us
    dot_general x6, matrix products, self_then_experts(): jnp.einsum('mnd,edh->mneh', normed, w_up, precision=PRECISE)  39.1 us
    psum x1, blocking collectives, on_device(): lax.psum((gain_grad, in_proj_grad, out_proj_grad, router_grad, up_grad, d...  37.6 us
  transfers between devices with their start and end apart: 1, of which 1 were waited for; matrix products, arithmetic and copies ran while one was open for 2% of the time, Pallas kernels for 0%

commit v1 on v0

v1 whole, which is shorter than its diff:
```python
import functools
import math

import jax
import jax.numpy as jnp
from jax import lax
from jax.experimental import pallas as pl
from jax.experimental.pallas import tpu as pltpu
from jax.sharding import PartitionSpec as P

MESH = pl.DeviceIdType.MESH
F32 = jnp.float32
BF16 = jnp.bfloat16
HEADS = 8
HEAD_DIM = 16
EPS = 1e-05
C1 = math.sqrt(2.0 / math.pi)
C2 = C1 * 0.044715
TILE = 512
MSG = 24


def nn(a, b):
    return jnp.dot(a, b, preferred_element_type=F32)


def nt(a, b):
    return lax.dot_general(a, b, (((1,), (1,)), ((), ())), preferred_element_type=F32)


def tn(a, b):
    return lax.dot_general(a, b, (((0,), (0,)), ((), ())), preferred_element_type=F32)


def split(x):
    high = x.astype(BF16)
    return high, (x - high.astype(F32)).astype(BF16)


def rows(*parts):
    return jnp.concatenate(parts, axis=0)


def cols(*parts):
    return jnp.concatenate(parts, axis=1)


def triple(w):
    high, low = split(w)
    return cols(high, low, high)


def k3(w3, x):
    high, low = x
    return nn(w3, rows(high, high, low))


def d3(w_high, w_low, x):
    high, low = x
    return nn(w_high, high) + (nn(w_low, high) + nn(w_high, low))


def outer(a, b):
    m, n = a[0].shape[0], b[0].shape[0]
    r = nt(rows(*a), rows(*b))
    return r[:m, :n] + (r[:m, n:] + r[m:, :n])


def wide(column, t):
    return cols(*([column] * (t // 128)))


def lanes(x):
    total = x[:, :128]
    for at in range(128, x.shape[1], 128):
        total = total + x[:, at : at + 128]
    return total


def by_head(x):
    return x.reshape(HEAD_DIM, HEADS, x.shape[-1])


def head_sum(x):
    return jnp.sum(by_head(x), axis=0)


def spread(r):
    return jnp.broadcast_to(r[None], (HEAD_DIM,) + r.shape).reshape(HEAD_DIM * HEADS, r.shape[-1])


def head_softmax(z):
    z = by_head(z)
    e = jnp.exp(z - jnp.max(z, axis=0)[None])
    p = e * (1.0 / jnp.sum(e, axis=0))[None]
    return p.reshape(HEAD_DIM * HEADS, p.shape[-1])


def softmax_back(p, dp):
    return p * (dp - spread(head_sum(p * dp)))


def mean(x):
    return jnp.sum(x, axis=0, keepdims=True) * (1.0 / x.shape[0])


def layer_norm(s, gain):
    centred = s - mean(s)
    r = lax.rsqrt(mean(centred * centred) + EPS)
    return centred * r * gain, r


def norm_back(dy, y, r, gain, inv_gain):
    xhat = y * inv_gain
    v = gain * dy
    return r * (v - mean(v) - xhat * mean(v * xhat)), dy * xhat


def put(ref, at, sl, x):
    d = x[0].shape[0]
    ref[at, 0:d, sl] = x[0]
    ref[at, d : 2 * d, sl] = x[1]


def get(ref, at, sl):
    both = ref[at, :, sl]
    d = both.shape[0] // 2
    return both[:d], both[d:]


def whole(x):
    return x[0].astype(F32) + x[1].astype(F32)


def gelu_parts(v):
    v2 = v * v
    g = 0.5 + 0.5 * jnp.tanh(v * (C1 + C2 * v2))
    return v2, g


def device_kernel(
    n_blk,
    features,
    func_points,
    coords,
    presence,
    valid,
    gain,
    in_proj,
    out_proj,
    router,
    up,
    down,
    cot,
    out,
    fgrad,
    g_gain,
    g_in,
    g_out,
    g_router,
    g_up,
    g_down,
    w_in,
    w_qc,
    w_self,
    w_out,
    w_outb,
    up_t,
    up_n,
    down_t,
    down_n,
    gcol,
    rgcol,
    fp,
    kc,
    vc,
    stream,
    y_ref,
    r_ref,
    qc,
    mixc,
    qs,
    ks,
    vs,
    mixs,
    dzq,
    inv_ref,
    rden_ref,
    gates,
    kv_t,
    kv_n,
    z_col,
    dkv_t,
    dkv_n,
    dz_col,
    acc_kv,
    acc_dkvc,
    acc_wi,
    acc_wo,
    acc_g,
    src_c,
    got_c,
    src_s,
    got_s,
    send_c,
    recv_c,
    send_s,
    recv_s,
):
    layers, experts, hid = up.shape[0], up.shape[1], up.shape[3]
    funcs, points = func_points.shape[1], func_points.shape[2]
    d = features.shape[2]
    count = features.shape[1]
    t = TILE
    tiles = count // t
    me = lax.axis_index("blk")

    barrier = pltpu.get_barrier_semaphore()
    for j in range(1, n_blk):
        pl.semaphore_signal(
            barrier, inc=1, device_id={"blk": lax.rem(me + j, n_blk)}, device_id_type=MESH
        )

    def copies(src, got, send, recv, at):
        return [
            pltpu.make_async_remote_copy(
                src_ref=src.at[at],
                dst_ref=got.at[at, j - 1],
                send_sem=send.at[at, j - 1],
                recv_sem=recv.at[at, j - 1],
                device_id={"blk": lax.rem(me + j, n_blk)},
                device_id_type=MESH,
            )
            for j in range(1, n_blk)
        ]

    def send_off(refs, at):
        for copy in copies(*refs, at):
            copy.start()

    def collect(refs, at):
        for copy in copies(*refs, at):
            copy.wait()
        src, got = refs[0], refs[1]
        total = src[at]
        for j in range(n_blk - 1):
            total = total + got[at, j]
        return total

    cross = (src_c, got_c, send_c, recv_c)
    own = (src_s, got_s, send_s, recv_s)

    head_mask = (
        lax.broadcasted_iota(jnp.int32, (HEADS, d), 0)
        == lax.broadcasted_iota(jnp.int32, (HEADS, d), 1) % HEADS
    ).astype(F32)
    spot = lax.broadcasted_iota(jnp.int32, (d, d), 0)
    perm = (
        lax.broadcasted_iota(jnp.int32, (d, d), 1) == (spot % HEADS) * HEAD_DIM + spot // HEADS
    ).astype(F32)
    perm16 = perm.astype(BF16)

    def compact(full):
        return jnp.sum(full.reshape(HEAD_DIM, HEADS, d) * head_mask[None], axis=1)

    def expand(compacted):
        full = jnp.broadcast_to(compacted[:, None, :], (HEAD_DIM, HEADS, d)) * head_mask[None]
        return full.reshape(d, d)

    def unpack(total, t_ref, n_ref, c_ref, at):
        full = expand(total[:HEAD_DIM])
        t_ref[at] = triple(full)
        n_ref[at] = triple(full.T)
        c_ref[at] = rows(*([total[HEAD_DIM:MSG]] * HEAD_DIM)).T

    for l in range(layers):
        for a in range(2):
            for j in range(3):
                w_high, w_low = split(in_proj[l, a, j])
                at = a * 3 + j
                high = nt(perm16, w_high).astype(BF16)
                low = nt(perm16, w_low).astype(BF16)
                w_in[l, at * d : (at + 1) * d, :] = cols(high, low, high)
                if (a, j) == (0, 0) or a == 1:
                    high = nt(w_high, perm16).astype(BF16)
                    low = nt(w_low, perm16).astype(BF16)
                    if a == 0:
                        w_qc[l] = cols(high, low, high)
                    else:
                        w_self[l, :, j * d : (j + 1) * d] = high
                        w_self[l, :, (3 + j) * d : (4 + j) * d] = low
            w_high, w_low = split(out_proj[l, a])
            contract = (((0,), (1,)), ((), ()))
            high = lax.dot_general(w_high, perm16, contract, preferred_element_type=F32).astype(BF16)
            low = lax.dot_general(w_low, perm16, contract, preferred_element_type=F32).astype(BF16)
            w_out[l, a] = cols(high, low, high)
            high = nn(perm16, w_high).astype(BF16)
            low = nn(perm16, w_low).astype(BF16)
            w_outb[l, a] = cols(high, low, high)
        for e in range(experts):
            lo, hi = e * hid, (e + 1) * hid
            w = up[l, e]
            high, low = split(w)
            up_n[l, :, lo:hi] = high
            up_n[l, :, experts * hid + lo : experts * hid + hi] = low
            up_t[l, lo:hi, :] = triple(w.T)
            w = down[l, e]
            down_n[l, lo:hi, :] = triple(w)
            high, low = split(w.T)
            down_t[l, :, lo:hi] = high
            down_t[l, :, experts * hid + lo : experts * hid + hi] = low
        for j in range(3):
            column = jnp.broadcast_to(gain[l, j : j + 1, :], (d, d)).T
            gcol[l * 3 + j] = column
            rgcol[l * 3 + j] = 1.0 / column

    present = [presence[0, f].astype(F32) for f in range(funcs)]
    all_present = present[0]
    for f in range(1, funcs):
        all_present = all_present + present[f]
    weight = [
        jnp.full((1, 1), present[f], F32) / jnp.full((1, 1), all_present, F32) for f in range(funcs)
    ]

    for f in range(funcs):
        high, low = split(func_points[0, f].T)
        fp[f, :d, :] = high
        fp[f, d:, :] = low

    ones = jnp.ones((16, points), BF16)
    ones_t = jnp.ones((16, t), BF16)

    def cross_summary(l):
        for f in range(funcs):
            both = fp[f]
            z = k3(w_in[l, d : 3 * d, :], (both[:d], both[d:]))
            kept = (
                lax.broadcasted_iota(jnp.int32, (1, points), 1) < valid[0, f, me]
            ).astype(F32)
            k = split(head_softmax(z[:d]) * kept)
            v = split(z[d:])
            put(kc, l * funcs + f, slice(None), k)
            put(vc, l * funcs + f, slice(None), v)
            r = nt(rows(*v, ones), rows(*k))
            src_c[l, f * MSG : f * MSG + HEAD_DIM, :] = compact(
                r[:d, :d] + (r[:d, d:] + r[d : 2 * d, :d])
            )
            src_c[l, f * MSG + HEAD_DIM : (f + 1) * MSG, :] = (
                r[2 * d : 2 * d + 8, :d] + r[2 * d : 2 * d + 8, d:]
            )
        send_off(cross, l)

    def cross_total(l):
        total = collect(cross, l)
        for f in range(funcs):
            unpack(
                total[f * MSG : (f + 1) * MSG],
                kv_t.at[l],
                kv_n.at[l],
                z_col.at[l],
                f,
            )

    def self_total(l):
        unpack(collect(own, l), kv_t.at[l], kv_n.at[l], z_col.at[l], funcs)

    def norm_in(l, at, s, sl):
        y, r = layer_norm(s, wide(gcol[l * 3 + at], t))
        y = split(y)
        put(y_ref, l * 3 + at, sl, y)
        r_ref[l * 3 + at, 0:1, sl] = r
        return y

    def norm_out(l, at, dy, sl):
        y = whole(get(y_ref, l * 3 + at, sl))
        ds, dg = norm_back(
            dy,
            y,
            r_ref[l * 3 + at, 0:1, sl],
            wide(gcol[l * 3 + at], t),
            wide(rgcol[l * 3 + at], t),
        )
        acc_g[l * 3 + at] += lanes(dg)
        return ds

    def cross_query(l, s, sl):
        y = norm_in(l, 0, s, sl)
        put(qc, l, sl, split(head_softmax(k3(w_in[l, :d, :], y))))

    def cross_read(l, s, sl):
        q2 = get(qc, l, sl)
        q = whole(q2)
        num = k3(kv_t[l, :funcs].reshape(funcs * d, 3 * d), q2)
        mix = q
        for f in range(funcs):
            rden = 1.0 / head_sum(q * wide(z_col[l, f], t))
            inv = rden * weight[f]
            inv_ref[l, f * 8 : (f + 1) * 8, sl] = inv
            inv_ref[l, (funcs + f) * 8 : (funcs + f + 1) * 8, sl] = rden
            mix = mix + num[f * d : (f + 1) * d] * spread(inv)
        mix = split(mix)
        put(mixc, l, sl, mix)
        s = s + k3(w_out[l, 0], mix)
        y = norm_in(l, 1, s, sl)
        z = k3(w_in[l, 3 * d :, :], y)
        q = split(head_softmax(z[:d]))
        k = split(head_softmax(z[d : 2 * d]))
        v = split(z[2 * d :])
        put(qs, l, sl, q)
        put(ks, l, sl, k)
        put(vs, l, sl, v)
        r = nt(rows(*v, ones_t), rows(*k))
        acc_kv[:d, :] += r[:d, :d] + (r[:d, d:] + r[d : 2 * d, :d])
        acc_kv[d:, :] += r[2 * d : 2 * d + 8, :d] + r[2 * d : 2 * d + 8, d:]
        stream[:, sl] = s

    def send_self(l):
        src_s[l, :HEAD_DIM, :] = compact(acc_kv[:d, :])
        src_s[l, HEAD_DIM:, :] = acc_kv[d:, :]
        send_off(own, l)

    def self_read(l, s, sl):
        q2 = get(qs, l, sl)
        q = whole(q2)
        num = k3(kv_t[l, funcs], q2)
        rden = 1.0 / head_sum(q * wide(z_col[l, funcs], t))
        rden_ref[l, :, sl] = rden
        mix = split(num * spread(rden) + q)
        put(mixs, l, sl, mix)
        s = s + k3(w_out[l, 1], mix)
        return s, norm_in(l, 2, s, sl)

    def hidden_in(l, e, y):
        return k3(up_t[l, e * hid : (e + 1) * hid, :], y)

    def down_of(l, e, x):
        at = experts * hid
        return d3(
            down_t[l, :, e * hid : (e + 1) * hid],
            down_t[l, :, at + e * hid : at + (e + 1) * hid],
            x,
        )

    def run_experts(l, y, sl):
        total = None
        for e in range(experts):
            v = hidden_in(l, e, y)
            _, g = gelu_parts(v)
            part = down_of(l, e, split(v * g * gates[l, e : e + 1, sl]))
            total = part if total is None else total + part
        return total

    def experts_back(l, ds, y, sl, forward):
        ds2 = split(ds)
        total, dy, dgate = None, None, []
        at = experts * hid
        for e in range(experts):
            gate = gates[l, e : e + 1, sl]
            v = hidden_in(l, e, y)
            back = k3(down_n[l, e * hid : (e + 1) * hid, :], ds2)
            v2, g = gelu_parts(v)
            act = v * g
            slope = g * (1.0 + (1.0 - g) * v * (2.0 * C1 + 6.0 * C2 * v2))
            dgate.append(jnp.sum(act * back, axis=0, keepdims=True))
            gated = split(act * gate)
            dpre = split(slope * back * gate)
            g_down[l, e] += outer(gated, ds2)
            g_up[l, e] += outer(y, dpre)
            if forward:
                part = down_of(l, e, gated)
                total = part if total is None else total + part
            part = d3(
                up_n[l, :, e * hid : (e + 1) * hid],
                up_n[l, :, at + e * hid : at + (e + 1) * hid],
                dpre,
            )
            dy = part if dy is None else dy + part
        probs = [gates[l, e : e + 1, sl] for e in range(experts)]
        centre = probs[0] * dgate[0]
        for e in range(1, experts):
            centre = centre + probs[e] * dgate[e]
        dlogit = rows(*[probs[e] * (dgate[e] - centre) for e in range(experts)])
        place = coords[0, :, sl]
        g_router[l] += lanes(rows(dlogit * place[0:1], dlogit * place[1:2]))
        return total, ds + norm_out(l, 2, dy, sl)

    def self_read_back(l, ds, sl):
        ds2 = split(ds)
        dmix = k3(w_outb[l, 1], ds2)
        acc_wo[l, 1] += outer(get(mixs, l, sl), ds2)
        back = k3(kv_n[l, funcs], split(dmix))
        q2 = get(qs, l, sl)
        q = whole(q2)
        rden = rden_ref[l, :, sl]
        u = rden * rden * head_sum(q * back)
        dq = dmix + spread(rden) * back - wide(z_col[l, funcs], t) * spread(u)
        put(dzq, 0, sl, split(softmax_back(q, dq)))
        da = split(dmix * spread(rden))
        u2 = split(u)
        r = nt(rows(*da, *u2), rows(*q2))
        acc_kv[:d, :] += r[:d, :d] + (r[:d, d:] + r[d : 2 * d, :d])
        low = r[2 * d :, :d] + r[2 * d :, d:]
        acc_kv[d:, :] += low[:8] + low[8:]

    def back_row(x):
        return jnp.broadcast_to(-jnp.sum(x * head_mask, axis=0, keepdims=True), (HEADS, d))

    def send_self_back(l):
        at = layers + l
        src_s[at, :HEAD_DIM, :] = compact(acc_kv[:d, :])
        src_s[at, HEAD_DIM:, :] = back_row(acc_kv[d:, :])
        send_off(own, at)

    def self_total_back(l):
        unpack(collect(own, layers + l), dkv_t, dkv_n, dz_col, 0)

    def attention_back(l, ds, sl):
        k2, v2 = get(ks, l, sl), get(vs, l, sl)
        dk = k3(dkv_n[0], v2) + wide(dz_col[0], t)
        dv = split(k3(dkv_t[0], k2))
        dzk = split(softmax_back(whole(k2), dk))
        q2 = get(dzq, 0, sl)
        dz = (rows(q2[0], dzk[0], dv[0]), rows(q2[1], dzk[1], dv[1]))
        y2 = get(y_ref, l * 3 + 1, sl)
        acc_wi[l, 3 * d :, :] += outer(dz, y2)
        dy = d3(w_self[l, :, : 3 * d], w_self[l, :, 3 * d :], dz)
        ds = ds + norm_out(l, 1, dy, sl)
        ds2 = split(ds)
        dmix = k3(w_outb[l, 0], ds2)
        acc_wo[l, 0] += outer(get(mixc, l, sl), ds2)
        back = k3(kv_n[l, :funcs].reshape(funcs * d, 3 * d), split(dmix))
        q2 = get(qc, l, sl)
        q = whole(q2)
        dq = dmix
        da, us = [], []
        for f in range(funcs):
            inv = inv_ref[l, f * 8 : (f + 1) * 8, sl]
            rden = inv_ref[l, (funcs + f) * 8 : (funcs + f + 1) * 8, sl]
            back_f = back[f * d : (f + 1) * d]
            u = inv * rden * head_sum(q * back_f)
            dq = dq + spread(inv) * back_f - wide(z_col[l, f], t) * spread(u)
            da.append(dmix * spread(inv))
            us.append(u)
        us.append(jnp.zeros_like(us[0]))
        side = rows(*us[:4])
        m = funcs * d
        r = nt(rows(*split(rows(*da)), *split(side)), rows(*q2))
        acc_dkvc[:m, :] += r[:m, :d] + (r[:m, d:] + r[m : 2 * m, :d])
        low = r[2 * m :, :d] + r[2 * m :, d:]
        acc_dkvc[m:, :] += (low[: 8 * (funcs + 1)] + low[8 * (funcs + 1) :])[: 8 * funcs]
        dz2 = split(softmax_back(q, dq))
        acc_wi[l, :d, :] += outer(dz2, get(y_ref, l * 3, sl))
        return ds + norm_out(l, 0, k3(w_qc[l], dz2), sl)

    def send_cross_back(l):
        at = layers + l
        for f in range(funcs):
            src_c[at, f * MSG : f * MSG + HEAD_DIM, :] = compact(acc_dkvc[f * d : (f + 1) * d, :])
            src_c[at, f * MSG + HEAD_DIM : (f + 1) * MSG, :] = back_row(
                acc_dkvc[funcs * d + f * 8 : funcs * d + (f + 1) * 8, :]
            )
        send_off(cross, at)

    def cross_keys_back(l):
        total = collect(cross, layers + l)
        for f in range(funcs):
            unpack(total[f * MSG : (f + 1) * MSG], dkv_t, dkv_n, dz_col, f)
        for f in range(funcs):
            k2 = get(kc, l * funcs + f, slice(None))
            v2 = get(vc, l * funcs + f, slice(None))
            dk = k3(dkv_n[f], v2) + wide(dz_col[f], points)
            dv = split(k3(dkv_t[f], k2))
            dzk = split(softmax_back(whole(k2), dk))
            both = fp[f]
            part = outer(
                (rows(dzk[0], dv[0]), rows(dzk[1], dv[1])), (both[:d], both[d:])
            )
            if f == 0:
                acc_wi[l, d : 3 * d, :] = part
            else:
                acc_wi[l, d : 3 * d, :] += part

    def each_tile(body):
        def step(i, carry):
            body(pl.ds(pl.multiple_of(i * t, t), t))
            return carry

        lax.fori_loop(0, tiles, step, 0)

    for ref in (acc_wi, acc_wo, acc_g, g_router, g_up, g_down):
        ref[...] = jnp.zeros_like(ref)
    acc_kv[...] = jnp.zeros_like(acc_kv)
    acc_dkvc[...] = jnp.zeros_like(acc_dkvc)
    pl.semaphore_wait(barrier, n_blk - 1)
    cross_summary(0)

    def first(sl):
        s = features[0, sl, :].T
        stream[:, sl] = s
        cross_query(0, s, sl)
        place = coords[0, :, sl]
        for l in range(layers):
            logit = [
                place[0:1] * router[l, 0, e] + place[1:2] * router[l, 1, e] for e in range(experts)
            ]
            top = functools.reduce(jnp.maximum, logit)
            grown = [jnp.exp(x - top) for x in logit]
            total = functools.reduce(jnp.add, grown)
            for e in range(experts):
                gates[l, e : e + 1, sl] = grown[e] / total

    each_tile(first)
    cross_summary(1)
    cross_total(0)
    each_tile(lambda sl: cross_read(0, stream[:, sl], sl))
    send_self(0)
    cross_total(1)
    acc_kv[...] = jnp.zeros_like(acc_kv)
    self_total(0)

    def second(sl):
        s, y = self_read(0, stream[:, sl], sl)
        s = s + run_experts(0, y, sl)
        cross_query(1, s, sl)
        cross_read(1, s, sl)

    each_tile(second)
    send_self(1)
    acc_kv[...] = jnp.zeros_like(acc_kv)
    self_total(1)

    def third(sl):
        s, y = self_read(1, stream[:, sl], sl)
        ds = cot[0, sl, :].T
        more, ds = experts_back(1, ds, y, sl, True)
        out[0, sl, :] = (s + more).T
        self_read_back(1, ds, sl)
        stream[:, sl] = ds

    each_tile(third)
    send_self_back(1)
    acc_kv[...] = jnp.zeros_like(acc_kv)
    self_total_back(1)

    def fourth(sl):
        ds = attention_back(1, stream[:, sl], sl)
        _, ds = experts_back(0, ds, get(y_ref, 2, sl), sl, False)
        self_read_back(0, ds, sl)
        stream[:, sl] = ds

    each_tile(fourth)
    send_self_back(0)
    send_cross_back(1)
    acc_dkvc[...] = jnp.zeros_like(acc_dkvc)
    self_total_back(0)

    def fifth(sl):
        fgrad[0, sl, :] = attention_back(0, stream[:, sl], sl).T

    each_tile(fifth)
    send_cross_back(0)
    cross_keys_back(1)
    cross_keys_back(0)

    exact = functools.partial(
        lax.dot_general, precision=lax.Precision.HIGHEST, preferred_element_type=F32
    )
    for l in range(layers):
        for a in range(2):
            for j in range(3):
                at = a * 3 + j
                g_in[l, a, j] = exact(
                    acc_wi[l, at * d : (at + 1) * d, :], perm, (((0,), (0,)), ((), ()))
                )
            g_out[l, a] = exact(perm, acc_wo[l, a], (((0,), (0,)), ((), ())))
        for j in range(3):
            g_gain[l, j : j + 1, :] = jnp.sum(acc_g[l * 3 + j].T, axis=0, keepdims=True)


def on_device(
    n_blk,
    features,
    func_points,
    coords,
    presence,
    valid_rows,
    norm_gain,
    in_proj,
    out_proj,
    router,
    expert_up,
    expert_down,
    cotangent,
):
    layers, experts, d, hid = expert_up.shape
    count = features.shape[1]
    funcs, points = func_points.shape[1], func_points.shape[2]
    wide_hid = experts * hid
    shape = jax.ShapeDtypeStruct
    vmem = pl.BlockSpec(memory_space=pltpu.VMEM)
    smem = pl.BlockSpec(memory_space=pltpu.SMEM)
    pair = pltpu.VMEM((layers, 2 * d, count), BF16)
    scratch = [
        pltpu.VMEM((layers, 6 * d, 3 * d), BF16),
        pltpu.VMEM((layers, d, 3 * d), BF16),
        pltpu.VMEM((layers, d, 6 * d), BF16),
        pltpu.VMEM((layers, 2, d, 3 * d), BF16),
        pltpu.VMEM((layers, 2, d, 3 * d), BF16),
        pltpu.VMEM((layers, wide_hid, 3 * d), BF16),
        pltpu.VMEM((layers, d, 2 * wide_hid), BF16),
        pltpu.VMEM((layers, d, 2 * wide_hid), BF16),
        pltpu.VMEM((layers, wide_hid, 3 * d), BF16),
        pltpu.VMEM((layers * 3, d, 128), F32),
        pltpu.VMEM((layers * 3, d, 128), F32),
        pltpu.VMEM((funcs, 2 * d, points), BF16),
        pltpu.VMEM((layers * funcs, 2 * d, points), BF16),
        pltpu.VMEM((layers * funcs, 2 * d, points), BF16),
        pltpu.VMEM((d, count), F32),
        pltpu.VMEM((layers * 3, 2 * d, count), BF16),
        pltpu.VMEM((layers * 3, 8, count), F32),
        pair,
        pair,
        pair,
        pair,
        pair,
        pair,
        pltpu.VMEM((1, 2 * d, count), BF16),
        pltpu.VMEM((layers, 2 * funcs * HEADS, count), F32),
        pltpu.VMEM((layers, HEADS, count), F32),
        pltpu.VMEM((layers, experts, count), F32),
        pltpu.VMEM((layers, funcs + 1, d, 3 * d), BF16),
        pltpu.VMEM((layers, funcs + 1, d, 3 * d), BF16),
        pltpu.VMEM((layers, funcs + 1, d, 128), F32),
        pltpu.VMEM((funcs, d, 3 * d), BF16),
        pltpu.VMEM((funcs, d, 3 * d), BF16),
        pltpu.VMEM((funcs, d, 128), F32),
        pltpu.VMEM((d + HEADS, d), F32),
        pltpu.VMEM((funcs * (d + HEADS), d), F32),
        pltpu.VMEM((layers, 6 * d, d), F32),
        pltpu.VMEM((layers, 2, d, d), F32),
        pltpu.VMEM((layers * 3, d, 128), F32),
        pltpu.VMEM((2 * layers, funcs * MSG, d), F32),
        pltpu.VMEM((2 * layers, n_blk - 1, funcs * MSG, d), F32),
        pltpu.VMEM((2 * layers, MSG, d), F32),
        pltpu.VMEM((2 * layers, n_blk - 1, MSG, d), F32),
    ] + [pltpu.SemaphoreType.DMA((2 * layers, n_blk - 1))] * 4
    results = pl.pallas_call(
        functools.partial(device_kernel, n_blk),
        out_shape=[
            shape(features.shape, F32),
            shape(features.shape, F32),
            shape(norm_gain.shape, F32),
            shape(in_proj.shape, F32),
            shape(out_proj.shape, F32),
            shape((layers, 2 * experts, 128), F32),
            shape(expert_up.shape, F32),
            shape(expert_down.shape, F32),
        ],
        in_specs=[vmem, vmem, vmem, smem, smem, vmem, vmem, vmem, smem, vmem, vmem, vmem],
        out_specs=[vmem] * 8,
        scratch_shapes=scratch,
        compiler_params=pltpu.CompilerParams(
            collective_id=0, has_side_effects=True, vmem_limit_bytes=62 * 2**20
        ),
        name="gnot",
    )(
        features,
        func_points,
        coords,
        presence,
        valid_rows,
        norm_gain,
        in_proj,
        out_proj,
        router,
        expert_up,
        expert_down,
        cotangent,
    )
    y, dx, gain_g, in_g, out_g, route_g, up_g, down_g = results
    route_g = jnp.sum(route_g, axis=-1).reshape(router.shape)
    return (y, dx) + lax.psum((gain_g, in_g, out_g, route_g, up_g, down_g), ("dp", "blk"))


def solution(mesh):
    placed = (
        P("dp", "blk", None),
        P("dp", None, "blk", None),
        P("dp", None, "blk"),
        P("dp", None),
        P("dp", None, None),
        P(),
        P(),
        P(),
        P(),
        P(),
        P(),
        P("dp", "blk", None),
    )
    return jax.shard_map(
        functools.partial(on_device, mesh.shape["blk"]),
        mesh=mesh,
        in_specs=placed,
        out_specs=(P("dp", "blk", None), P("dp", "blk", None), P(), P(), P(), P(), P(), P()),
        check_vma=False,
    )
```

time: 1400 us -> 286 us (0.20)
  blocking collectives: 784 us -> 40.4 us
  matrix products: 300 us -> 0 us
  other arithmetic: 162 us -> 0.09 us
  Pallas kernels: 0 us -> 123 us
  local copies, waits for them, and re-layouts: 49 us -> 11.3 us
  waiting for transfers between devices: 74.5 us -> 97.2 us
    all_gather x16 -> x0, blocking collectives: 525 us -> none  [carried_in(): pieces = jax.tree.map(lambda part: lax.all_gather(part, axis), value)]
    dot_general x96 -> x0, matrix products: 300 us -> none  [the longest x44 83.5 us: linear(): return jnp.dot(matrix, weight, precision=PRECISE)]
    psum x7 -> x1, blocking collectives: 259 us -> 40.4 us  [on_device(): lax.psum((gain_g, in_g, out_g, route_g, up_g, down_g), ('dp', 'blk'))]
    pallas_call x0 -> x1, Pallas kernels: none -> 123 us  [on_device(): pl.pallas_call(functools.partial(device_kernel, n_blk), out_shape=[shape(...]
    select_n x112 -> x0, other arithmetic: 98.2 us -> none  [turn(): jnp.where(position < mine, new, old)]
    reduce_sum x31 -> x1, other arithmetic: 22.7 us -> 0.09 us  [on_device(): route_g = jnp.sum(route_g, axis=-1).reshape(router.shape)]
    psum x1, waiting for transfers between devices: 74.5 us -> 97.1 us  [on_device(): lax.psum((gain_g, in_g, out_g, route_g, up_g, down_g), ('dp', 'blk'))]
    another operation x34 -> x0, other arithmetic: 22.1 us -> none
  transfers between devices with their start and end apart: 1 -> 1, of which waited for: 1 -> 1; matrix products, arithmetic and copies ran while one was open for 2% -> 0% of each run, Pallas kernels for 0% -> 0%
where the time goes in v1:
time: 286 us
  Pallas kernels  123 us (43%)
  waiting for transfers between devices  97.2 us (34%)
  blocking collectives  40.4 us (14%)
  between operations  14.1 us (5%)
  local copies, waits for them, and re-layouts  11.3 us (4%)
    pallas_call x1, Pallas kernels, on_device(): pl.pallas_call(functools.partial(device_kernel, n_blk), out_shape=[shape(...  123 us
    psum x1, waiting for transfers between devices, on_device(): lax.psum((gain_g, in_g, out_g, route_g, up_g, down_g), ('dp', 'blk'))  97.1 us
    psum x1, blocking collectives, on_device(): lax.psum((gain_g, in_g, out_g, route_g, up_g, down_g), ('dp', 'blk'))  40.4 us
    unnamed x27, local copies, waits for them, and re-layouts  11.2 us
  transfers between devices with their start and end apart: 1, of which 1 were waited for; matrix products, arithmetic and copies ran while one was open for 0% of the time, Pallas kernels for 0%

profile of v1, /device:TPU:0, one launch (start us, length us, event | category | flops | bytes accessed | tf_op | source)
XLA Modules:
  0.0 286.0 jit_solution(11036826667415858936)
XLA Ops:
  7.2 0.0 copy-start.8
  7.2 0.0 all-reduce.4.cloned.1.call-start
  7.2 1.3 copy.20.valid
  8.5 0.0 copy-done.8
  8.5 0.6 copy.21.gain
  9.1 123.0 %gnot.1 = (f32[1,2048,128]{2,1,0:T(8,128)}, f32[1,2048,128]{2,1,0:T(8,128)}, f32[2,3,128]{2,1,0:T(4,128)}, f32[2,2,3,128,128]{4,3,2,1,0:T(8,128)}, f32[2,2,128,1...) custom-call(f32[1,2048,128]{2,1,0:T(8,128)} %features.1, ...), custom_call_target="tpu_custom_call" | custom-call | tf_op jit(solution)/shard_map/gnot/pallas_call | solution.py:747
  132.1 0.0 copy-start.6
  132.1 0.0 copy-start.1
  132.1 0.0 all-reduce.4.cloned.1.call-update
  132.1 0.7 copy-done.6
  132.8 0.1 reduce_sum.9
  132.9 0.0 copy-start.7
  132.9 0.1 reshape.19
  132.9 0.6 copy-done.7
  133.5 40.4 %all-reduce = (f32[2,3,128]{2,1,0:T(4,128)S(1)}, f32[2,2,4]{2,1,0:T(2,128)}) all-reduce(f32[2,3,128]{2,1,0:T(4,128)S(1)} %copy-done.7, f32[2,2,4]{2,1,0:T(2,128)S(1)} %reshape.19), channel_id=1, replica_groups=mesh['dp'=4,'blk'=8] {'dp','blk'}, use_global_device_ids=true, to_apply=%region_0.0 | all-reduce | flops 784 | bytes 6272 | tf_op jit(solution)/shard_map/psum | solution.py:782
  173.9 0.6 copy.22
  174.5 97.1 %all-reduce.4.cloned.1.call-done = (f32[2,2,3,128,128]{4,3,2,1,0:T(8,128)}, f32[2,2,128,128]{3,2,1,0:T(8,128)}, f32[2,4,128,256]{3,2,1,0:T(8,128)}, f32[2,4,256,128]{3,2,1,0:T(8,128)}) async-done(((f32[2,2,3,128,128]{4,3,2,1,0:T(8,128)}, f32[2,2,128,128]{3,2,1,0:T(8,128)}, f32[2,4,128,256]{3,2,1,0:T(8,128)}, f32[2,4,256,128]{3,2,1,0:T(8,128)}), (f32[2,2,3,128,128]{4,3,2,1,0:T(8,128)}, ...) | async-done | bytes 3145744 | tf_op jit(solution)/shard_map/psum | solution.py:782
  271.6 0.0 copy-done.1
  271.7 0.0 copy-start
  271.7 1.0 copy.33
  272.6 0.6 copy-done
  273.3 0.0 copy-start.4
  273.3 1.0 copy.34
  274.2 0.5 copy-done.4
  274.8 0.0 copy-start.5
  274.8 0.0 copy-start.3
  274.8 0.9 copy.35
  275.7 0.2 copy-done.5
  275.9 0.7 copy.36
  276.6 0.0 copy-done.3
  276.6 0.0 copy-start.2
  276.6 1.0 copy.37
  277.5 0.6 copy-done.2
  278.2 1.0 copy.38
Async XLA Ops:
  7.2 1.3 copy-start.8
  7.2 264.5 %all-reduce.4.cloned.1.call-start = ((), (), s32[]{:S(2)}) async-start(), calls=%async_computation | async-start | bytes 6291456 | tf_op jit(solution)/shard_map/psum | solution.py:782
  132.1 0.7 copy-start.6
  132.1 139.6 %copy-start.1 = (f32[1,2048,128]{2,1,0:T(8,128)S(1)}, f32[1,2048,128]{2,1,0:T(8,128)}, u32[]{:S(2)}) copy-start(f32[1,2048,128]{2,1,0:T(8,128)} %get-tuple-element.46) | copy-start | bytes 3145732
  132.9 0.7 copy-start.7
  271.7 1.6 copy-start
  273.3 1.5 copy-start.4
  274.8 1.1 copy-start.5
  274.8 1.8 copy-start.3
  276.6 1.6 copy-start.2
Sparse Core Ops, SparseCore 0:
  132.2 139.3 all-reduce.3

commit v2 on v1

--- a/solution.py
+++ b/solution.py
@@ -16,7 +16,7 @@
 EPS = 1e-05
 C1 = math.sqrt(2.0 / math.pi)
 C2 = C1 * 0.044715
-TILE = 512
+TILE = 1024
 MSG = 24
 
 
@@ -139,27 +139,33 @@
 
 
 def device_kernel(
+    n_dp,
     n_blk,
-    features,
-    func_points,
+    summed,
+    features_hbm,
+    points_hbm,
     coords,
     presence,
     valid,
     gain,
-    in_proj,
-    out_proj,
+    in_hbm,
+    out_hbm,
     router,
-    up,
-    down,
-    cot,
+    up_hbm,
+    down_hbm,
+    cot_hbm,
     out,
     fgrad,
-    g_gain,
-    g_in,
-    g_out,
-    g_router,
+    f_att,
+    f_up,
+    f_down,
+    f_small,
+    points_ref,
+    load_sem,
+    g_att,
     g_up,
     g_down,
+    g_small,
     w_in,
     w_qc,
     w_self,
@@ -198,6 +204,9 @@
     acc_wi,
     acc_wo,
     acc_g,
+    acc_r,
+    dy_ref,
+    dgate_ref,
     src_c,
     got_c,
     src_s,
@@ -206,20 +215,233 @@
     recv_c,
     send_s,
     recv_s,
+    *ring,
 ):
-    layers, experts, hid = up.shape[0], up.shape[1], up.shape[3]
-    funcs, points = func_points.shape[1], func_points.shape[2]
-    d = features.shape[2]
-    count = features.shape[1]
-    t = TILE
-    tiles = count // t
+    if not summed:
+        g_att, g_up, g_down, g_small = f_att, f_up, f_down, f_small
+    layers, experts, hid = router.shape[0], router.shape[2], up_hbm.shape[2]
+    funcs, points = points_hbm.shape[1], points_hbm.shape[2]
+    count, d = features_hbm.shape[1:]
+
+    def load(src, dst, at):
+        copy = pltpu.make_async_copy(src, dst, load_sem.at[at])
+        copy.start()
+        return copy
+
+    att_loads = []
+    for at in range(layers * 2):
+        att_loads.append(load(in_hbm.at[at], f_att.at[at, pl.ds(0, 3 * d)], 2 * at))
+        att_loads.append(load(out_hbm.at[at], f_att.at[at, pl.ds(3 * d, d)], 2 * at + 1))
+    at = 4 * layers
+    points_load = load(points_hbm, points_ref, at)
+    features_load = load(features_hbm, out, at + 1)
+    up_load = load(up_hbm, f_up, at + 2)
+    down_load = load(down_hbm, f_down, at + 3)
+    cot_load = load(cot_hbm, fgrad, at + 4)
     me = lax.axis_index("blk")
-
+    own_dp = lax.axis_index("dp")
+    n_flat, n_line = n_dp, n_blk // 2
+    core, line = own_dp % 2, me // 2
+    flat = (own_dp // 2) * 2 + me % 2
+
+    sibling = {"dp": own_dp - core + (1 - core), "blk": me}
+
+    def flat_at(j):
+        at = lax.rem(flat + j, n_flat)
+        return {"dp": (at // 2) * 2 + core, "blk": line * 2 + at % 2}
+
+    def line_at(j):
+        return {"dp": own_dp, "blk": lax.rem(line + j, n_line) * 2 + me % 2}
+
+    partners = [{"dp": own_dp, "blk": lax.rem(me + j, n_blk)} for j in range(1, n_blk)]
+    if summed:
+        partners += [sibling] + [flat_at(j) for j in range(1, n_flat)]
     barrier = pltpu.get_barrier_semaphore()
-    for j in range(1, n_blk):
-        pl.semaphore_signal(
-            barrier, inc=1, device_id={"blk": lax.rem(me + j, n_blk)}, device_id_type=MESH
+    for partner in partners:
+        pl.semaphore_signal(barrier, inc=1, device_id=partner, device_id_type=MESH)
+
+    running = []
+
+    def take():
+        now = [steps.pop(0) for steps in running]
+        running[:] = [steps for steps in running if steps]
+
+        def run():
+            for step in now:
+                step()
+
+        return run
+
+    def tick():
+        take()()
+
+    def made(jobs, send, recv):
+        return [
+            pltpu.make_async_remote_copy(
+                src_ref=src,
+                dst_ref=dst,
+                send_sem=send.at[k],
+                recv_sem=recv.at[k],
+                device_id=device,
+                device_id_type=MESH,
+            )
+            for k, src, dst, device in jobs()
+        ]
+
+    def go(jobs, send, recv):
+        for copy in made(jobs, send, recv):
+            copy.start()
+
+    def settle(jobs, send, recv):
+        for copy in made(jobs, send, recv):
+            copy.wait()
+
+    def reduction(local, final, halves, parts, pieces, send, recv):
+        half = local.shape[0] // 2
+        part = half // n_flat
+        piece = part // n_line
+
+        def at(start, size):
+            return pl.ds(pl.multiple_of(start, 8), size)
+
+        def of_core(other=0):
+            return at((core if not other else 1 - core) * half, half)
+
+        def of_flat(j=0):
+            return at(core * half + lax.rem(flat + j, n_flat) * part, part)
+
+        def of_line(j=0):
+            return at(core * half + flat * part + lax.rem(line + j, n_line) * piece, piece)
+
+        k1 = 1
+        k2 = k1 + n_flat - 1
+        k3_ = k2 + n_line - 1
+        k4 = k3_ + n_line - 1
+        k5 = k4 + n_flat - 1
+
+        def core_out():
+            return [(0, local.at[of_core(1)], halves, sibling)]
+
+        def flat_out():
+            return [
+                (k1 + j - 1, local.at[of_flat(j)], parts.at[j - 1], flat_at(j))
+                for j in range(1, n_flat)
+            ]
+
+        def line_out():
+            return [
+                (k2 + j - 1, local.at[of_line(j)], pieces.at[j - 1], line_at(j))
+                for j in range(1, n_line)
+            ]
+
+        def line_back():
+            mine = final.at[of_line()]
+            return [(k3_ + j - 1, mine, mine, line_at(j)) for j in range(1, n_line)]
+
+        def flat_back():
+            mine = final.at[of_flat()]
+            return [(k4 + j - 1, mine, mine, flat_at(j)) for j in range(1, n_flat)]
+
+        def core_back():
+            mine = final.at[of_core()]
+            return [(k5, mine, mine, sibling)]
+
+        def one():
+            go(core_out, send, recv)
+
+        def two():
+            settle(core_out, send, recv)
+            spot = of_core()
+            local[spot] = local[spot] + halves[...]
+            go(flat_out, send, recv)
+
+        def three():
+            settle(flat_out, send, recv)
+            spot = of_flat()
+            total = local[spot]
+            for j in range(n_flat - 1):
+                total = total + parts[j]
+            local[spot] = total
+            go(line_out, send, recv)
+
+        def four():
+            settle(line_out, send, recv)
+            spot = of_line()
+            total = local[spot]
+            for j in range(n_line - 1):
+                total = total + pieces[j]
+            final[spot] = total
+            go(line_back, send, recv)
+
+        def five():
+            settle(line_back, send, recv)
+            go(flat_back, send, recv)
+
+        def six():
+            settle(flat_back, send, recv)
+            go(core_back, send, recv)
+
+        def seven():
+            settle(core_back, send, recv)
+
+        return [one, two, three, four, five, six, seven]
+
+    def exchange_small(local, final, held, send, recv):
+        levels = (
+            (0, 2, core, lambda: [sibling], 0),
+            (2, n_flat, flat, lambda: [flat_at(j) for j in range(1, n_flat)], 1),
+            (2 + n_flat, n_line, line, lambda: [line_at(j) for j in range(1, n_line)], n_flat),
         )
+
+        def jobs_of(level):
+            at, _, place, devices, k = levels[level]
+
+            def jobs():
+                mine = held.at[at + place]
+                return [(k + j, mine, mine, device) for j, device in enumerate(devices())]
+
+            return jobs
+
+        def start(level, value):
+            at, _, place, _, _ = levels[level]
+            held[at + place] = value
+            go(jobs_of(level), send, recv)
+
+        def finish(level):
+            settle(jobs_of(level), send, recv)
+            at, size = levels[level][:2]
+            value = held[at]
+            for j in range(1, size):
+                value = value + held[at + j]
+            return value
+
+        def last():
+            final[...] = finish(2)
+
+        return [
+            lambda: start(0, local[...]),
+            lambda: start(1, finish(0)),
+            lambda: start(2, finish(1)),
+            last,
+        ]
+
+    def reduce_up(l, pair):
+        seg = l * 2 + pair
+        running.append(
+            reduction(g_up.at[seg], f_up.at[seg], *[ref.at[seg] for ref in ring[:5]])
+        )
+
+    def reduce_rows(seg, local, final):
+        running.append(reduction(local, final, *[ref.at[seg] for ref in ring[5:10]]))
+
+    def reduce_pair(l, pair):
+        if summed:
+            reduce_up(l, pair)
+            reduce_rows(l * 2 + pair, g_down.at[l * 2 + pair], f_down.at[l * 2 + pair])
+
+    def reduce_att(l, a):
+        if summed:
+            reduce_rows(layers * 2 + l * 2 + a, g_att.at[l * 2 + a], f_att.at[l * 2 + a])
 
     def copies(src, got, send, recv, at):
         return [
@@ -273,42 +495,56 @@
         n_ref[at] = triple(full.T)
         c_ref[at] = rows(*([total[HEAD_DIM:MSG]] * HEAD_DIM)).T
 
+    def cut_attention():
+        for copy in att_loads:
+            copy.wait()
+        for l in range(layers):
+            for a in range(2):
+                for j in range(3):
+                    w_high, w_low = split(f_att[l * 2 + a, j * d : (j + 1) * d, :])
+                    at = a * 3 + j
+                    high = nt(perm16, w_high).astype(BF16)
+                    low = nt(perm16, w_low).astype(BF16)
+                    w_in[l, at * d : (at + 1) * d, :] = cols(high, low, high)
+                    if (a, j) == (0, 0) or a == 1:
+                        high = nt(w_high, perm16).astype(BF16)
+                        low = nt(w_low, perm16).astype(BF16)
+                        if a == 0:
+                            w_qc[l] = cols(high, low, high)
+                        else:
+                            w_self[l, :, j * d : (j + 1) * d] = high
+                            w_self[l, :, (3 + j) * d : (4 + j) * d] = low
+                w_high, w_low = split(f_att[l * 2 + a, 3 * d :, :])
+                contract = (((0,), (1,)), ((), ()))
+                high, low = [
+                    lax.dot_general(w, perm16, contract, preferred_element_type=F32).astype(BF16)
+                    for w in (w_high, w_low)
+                ]
+                w_out[l, a] = cols(high, low, high)
+                high = nn(perm16, w_high).astype(BF16)
+                low = nn(perm16, w_low).astype(BF16)
+                w_outb[l, a] = cols(high, low, high)
+
+    def cut_experts():
+        up_load.wait()
+        down_load.wait()
+        for l in range(layers):
+            for e in range(experts):
+                lo, hi = e * hid, (e + 1) * hid
+                seg, spot = l * 2 + e // 2, e % 2
+                w = f_up[seg, spot * d : (spot + 1) * d, :]
+                high, low = split(w)
+                up_n[l, :, lo:hi] = high
+                up_n[l, :, experts * hid + lo : experts * hid + hi] = low
+                up_t[l, lo:hi, :] = triple(w.T)
+                w = f_down[seg, spot * hid : (spot + 1) * hid, :]
+                down_n[l, lo:hi, :] = triple(w)
+                high, low = split(w.T)
+                down_t[l, :, lo:hi] = high
+                down_t[l, :, experts * hid + lo : experts * hid + hi] = low
+
+    cut_attention()
     for l in range(layers):
-        for a in range(2):
-            for j in range(3):
-                w_high, w_low = split(in_proj[l, a, j])
-                at = a * 3 + j
-                high = nt(perm16, w_high).astype(BF16)
-                low = nt(perm16, w_low).astype(BF16)
-                w_in[l, at * d : (at + 1) * d, :] = cols(high, low, high)
-                if (a, j) == (0, 0) or a == 1:
-                    high = nt(w_high, perm16).astype(BF16)
-                    low = nt(w_low, perm16).astype(BF16)
-                    if a == 0:
-                        w_qc[l] = cols(high, low, high)
-                    else:
-                        w_self[l, :, j * d : (j + 1) * d] = high
-                        w_self[l, :, (3 + j) * d : (4 + j) * d] = low
-            w_high, w_low = split(out_proj[l, a])
-            contract = (((0,), (1,)), ((), ()))
-            high = lax.dot_general(w_high, perm16, contract, preferred_element_type=F32).astype(BF16)
-            low = lax.dot_general(w_low, perm16, contract, preferred_element_type=F32).astype(BF16)
-            w_out[l, a] = cols(high, low, high)
-            high = nn(perm16, w_high).astype(BF16)
-            low = nn(perm16, w_low).astype(BF16)
-            w_outb[l, a] = cols(high, low, high)
-        for e in range(experts):
-            lo, hi = e * hid, (e + 1) * hid
-            w = up[l, e]
-            high, low = split(w)
-            up_n[l, :, lo:hi] = high
-            up_n[l, :, experts * hid + lo : experts * hid + hi] = low
-            up_t[l, lo:hi, :] = triple(w.T)
-            w = down[l, e]
-            down_n[l, lo:hi, :] = triple(w)
-            high, low = split(w.T)
-            down_t[l, :, lo:hi] = high
-            down_t[l, :, experts * hid + lo : experts * hid + hi] = low
         for j in range(3):
             column = jnp.broadcast_to(gain[l, j : j + 1, :], (d, d)).T
             gcol[l * 3 + j] = column
@@ -322,13 +558,13 @@
         jnp.full((1, 1), present[f], F32) / jnp.full((1, 1), all_present, F32) for f in range(funcs)
     ]
 
+    points_load.wait()
     for f in range(funcs):
-        high, low = split(func_points[0, f].T)
+        high, low = split(points_ref[0, f].T)
         fp[f, :d, :] = high
         fp[f, d:, :] = low
 
     ones = jnp.ones((16, points), BF16)
-    ones_t = jnp.ones((16, t), BF16)
 
     def cross_summary(l):
         for f in range(funcs):
@@ -365,7 +601,7 @@
         unpack(collect(own, l), kv_t.at[l], kv_n.at[l], z_col.at[l], funcs)
 
     def norm_in(l, at, s, sl):
-        y, r = layer_norm(s, wide(gcol[l * 3 + at], t))
+        y, r = layer_norm(s, wide(gcol[l * 3 + at], sl.size))
         y = split(y)
         put(y_ref, l * 3 + at, sl, y)
         r_ref[l * 3 + at, 0:1, sl] = r
@@ -377,8 +613,8 @@
             dy,
             y,
             r_ref[l * 3 + at, 0:1, sl],
-            wide(gcol[l * 3 + at], t),
-            wide(rgcol[l * 3 + at], t),
+            wide(gcol[l * 3 + at], sl.size),
+            wide(rgcol[l * 3 + at], sl.size),
         )
         acc_g[l * 3 + at] += lanes(dg)
         return ds
@@ -393,7 +629,7 @@
         num = k3(kv_t[l, :funcs].reshape(funcs * d, 3 * d), q2)
         mix = q
         for f in range(funcs):
-            rden = 1.0 / head_sum(q * wide(z_col[l, f], t))
+            rden = 1.0 / head_sum(q * wide(z_col[l, f], sl.size))
             inv = rden * weight[f]
             inv_ref[l, f * 8 : (f + 1) * 8, sl] = inv
             inv_ref[l, (funcs + f) * 8 : (funcs + f + 1) * 8, sl] = rden
@@ -409,7 +645,7 @@
         put(qs, l, sl, q)
         put(ks, l, sl, k)
         put(vs, l, sl, v)
-        r = nt(rows(*v, ones_t), rows(*k))
+        r = nt(rows(*v, jnp.ones((16, sl.size), BF16)), rows(*k))
         acc_kv[:d, :] += r[:d, :d] + (r[:d, d:] + r[d : 2 * d, :d])
         acc_kv[d:, :] += r[2 * d : 2 * d + 8, :d] + r[2 * d : 2 * d + 8, d:]
         stream[:, sl] = s
@@ -423,7 +659,7 @@
         q2 = get(qs, l, sl)
         q = whole(q2)
         num = k3(kv_t[l, funcs], q2)
-        rden = 1.0 / head_sum(q * wide(z_col[l, funcs], t))
+        rden = 1.0 / head_sum(q * wide(z_col[l, funcs], sl.size))
         rden_ref[l, :, sl] = rden
         mix = split(num * spread(rden) + q)
         put(mixs, l, sl, mix)
@@ -450,39 +686,47 @@
             total = part if total is None else total + part
         return total
 
-    def experts_back(l, ds, y, sl, forward):
-        ds2 = split(ds)
-        total, dy, dgate = None, None, []
+    def expert_back(l, e, y, ds2, sl):
         at = experts * hid
-        for e in range(experts):
-            gate = gates[l, e : e + 1, sl]
-            v = hidden_in(l, e, y)
-            back = k3(down_n[l, e * hid : (e + 1) * hid, :], ds2)
-            v2, g = gelu_parts(v)
-            act = v * g
-            slope = g * (1.0 + (1.0 - g) * v * (2.0 * C1 + 6.0 * C2 * v2))
-            dgate.append(jnp.sum(act * back, axis=0, keepdims=True))
-            gated = split(act * gate)
-            dpre = split(slope * back * gate)
-            g_down[l, e] += outer(gated, ds2)
-            g_up[l, e] += outer(y, dpre)
-            if forward:
-                part = down_of(l, e, gated)
-                total = part if total is None else total + part
-            part = d3(
-                up_n[l, :, e * hid : (e + 1) * hid],
-                up_n[l, :, at + e * hid : at + (e + 1) * hid],
-                dpre,
-            )
-            dy = part if dy is None else dy + part
+        gate = gates[l, e : e + 1, sl]
+        v = hidden_in(l, e, y)
+        back = k3(down_n[l, e * hid : (e + 1) * hid, :], ds2)
+        v2, g = gelu_parts(v)
+        act = v * g
+        slope = g * (1.0 + (1.0 - g) * v * (2.0 * C1 + 6.0 * C2 * v2))
+        dgate_ref[e : e + 1, sl] = jnp.sum(act * back, axis=0, keepdims=True)
+        gated = split(act * gate)
+        dpre = split(slope * back * gate)
+        seg, spot = l * 2 + e // 2, e % 2
+        g_down[seg, spot * hid : (spot + 1) * hid, :] += outer(gated, ds2)
+        g_up[seg, spot * d : (spot + 1) * d, :] += outer(y, dpre)
+        dy = d3(
+            up_n[l, :, e * hid : (e + 1) * hid],
+            up_n[l, :, at + e * hid : at + (e + 1) * hid],
+            dpre,
+        )
+        return gated, dy
+
+    def gates_back(l, ds, dy, sl):
         probs = [gates[l, e : e + 1, sl] for e in range(experts)]
+        dgate = [dgate_ref[e : e + 1, sl] for e in range(experts)]
         centre = probs[0] * dgate[0]
         for e in range(1, experts):
             centre = centre + probs[e] * dgate[e]
         dlogit = rows(*[probs[e] * (dgate[e] - centre) for e in range(experts)])
         place = coords[0, :, sl]
-        g_router[l] += lanes(rows(dlogit * place[0:1], dlogit * place[1:2]))
-        return total, ds + norm_out(l, 2, dy, sl)
+        acc_r[l] += lanes(rows(dlogit * place[0:1], dlogit * place[1:2]))
+        return ds + norm_out(l, 2, dy, sl)
+
+    def experts_both(l, ds, y, sl):
+        ds2 = split(ds)
+        total, dy = None, None
+        for e in range(experts):
+            gated, part = expert_back(l, e, y, ds2, sl)
+            dy = part if dy is None else dy + part
+            part = down_of(l, e, gated)
+            total = part if total is None else total + part
+        return total, gates_back(l, ds, dy, sl)
 
     def self_read_back(l, ds, sl):
         ds2 = split(ds)
@@ -493,7 +737,7 @@
         q = whole(q2)
         rden = rden_ref[l, :, sl]
         u = rden * rden * head_sum(q * back)
-        dq = dmix + spread(rden) * back - wide(z_col[l, funcs], t) * spread(u)
+        dq = dmix + spread(rden) * back - wide(z_col[l, funcs], sl.size) * spread(u)
         put(dzq, 0, sl, split(softmax_back(q, dq)))
         da = split(dmix * spread(rden))
         u2 = split(u)
@@ -516,7 +760,7 @@
 
     def attention_back(l, ds, sl):
         k2, v2 = get(ks, l, sl), get(vs, l, sl)
-        dk = k3(dkv_n[0], v2) + wide(dz_col[0], t)
+        dk = k3(dkv_n[0], v2) + wide(dz_col[0], sl.size)
         dv = split(k3(dkv_t[0], k2))
         dzk = split(softmax_back(whole(k2), dk))
         q2 = get(dzq, 0, sl)
@@ -524,7 +768,9 @@
         y2 = get(y_ref, l * 3 + 1, sl)
         acc_wi[l, 3 * d :, :] += outer(dz, y2)
         dy = d3(w_self[l, :, : 3 * d], w_self[l, :, 3 * d :], dz)
-        ds = ds + norm_out(l, 1, dy, sl)
+        return ds + norm_out(l, 1, dy, sl)
+
+    def cross_read_back(l, ds, sl):
         ds2 = split(ds)
         dmix = k3(w_outb[l, 0], ds2)
         acc_wo[l, 0] += outer(get(mixc, l, sl), ds2)
@@ -538,17 +784,22 @@
             rden = inv_ref[l, (funcs + f) * 8 : (funcs + f + 1) * 8, sl]
             back_f = back[f * d : (f + 1) * d]
             u = inv * rden * head_sum(q * back_f)
-            dq = dq + spread(inv) * back_f - wide(z_col[l, f], t) * spread(u)
+            dq = dq + spread(inv) * back_f - wide(z_col[l, f], sl.size) * spread(u)
             da.append(dmix * spread(inv))
             us.append(u)
-        us.append(jnp.zeros_like(us[0]))
-        side = rows(*us[:4])
+        if funcs % 2:
+            us.append(jnp.zeros_like(us[0]))
+        side = rows(*us)
         m = funcs * d
         r = nt(rows(*split(rows(*da)), *split(side)), rows(*q2))
         acc_dkvc[:m, :] += r[:m, :d] + (r[:m, d:] + r[m : 2 * m, :d])
         low = r[2 * m :, :d] + r[2 * m :, d:]
-        acc_dkvc[m:, :] += (low[: 8 * (funcs + 1)] + low[8 * (funcs + 1) :])[: 8 * funcs]
-        dz2 = split(softmax_back(q, dq))
+        high = side.shape[0]
+        acc_dkvc[m:, :] += (low[:high] + low[high:])[: 8 * funcs]
+        return softmax_back(q, dq)
+
+    def cross_query_back(l, ds, dz, sl):
+        dz2 = split(dz)
         acc_wi[l, :d, :] += outer(dz2, get(y_ref, l * 3, sl))
         return ds + norm_out(l, 0, k3(w_qc[l], dz2), sl)
 
@@ -580,22 +831,46 @@
             else:
                 acc_wi[l, d : 3 * d, :] += part
 
-    def each_tile(body):
+    def each_tile(body, tile=TILE, ticks=()):
+        tile = min(tile, count)
+        if tile == count:
+            body(pl.ds(0, count))
+            return
+
+        moves = [(at, take()) for at in ticks]
+
         def step(i, carry):
-            body(pl.ds(pl.multiple_of(i * t, t), t))
+            for at, move in moves:
+                pl.when(i == at)(move)
+            body(pl.ds(pl.multiple_of(i * tile, tile), tile))
             return carry
 
-        lax.fori_loop(0, tiles, step, 0)
-
-    for ref in (acc_wi, acc_wo, acc_g, g_router, g_up, g_down):
+        lax.fori_loop(0, count // tile, step, 0)
+
+    exact = functools.partial(
+        lax.dot_general, precision=lax.Precision.HIGHEST, preferred_element_type=F32
+    )
+
+    def finish_in(l, a, j):
+        at = a * 3 + j
+        g_att[l * 2 + a, j * d : (j + 1) * d, :] = exact(
+            acc_wi[l, at * d : (at + 1) * d, :], perm, (((0,), (0,)), ((), ()))
+        )
+
+    def finish_out(l, a):
+        g_att[l * 2 + a, 3 * d :, :] = exact(perm, acc_wo[l, a], (((0,), (0,)), ((), ())))
+
+    for ref in (acc_wi, acc_wo, acc_g, acc_r):
         ref[...] = jnp.zeros_like(ref)
     acc_kv[...] = jnp.zeros_like(acc_kv)
     acc_dkvc[...] = jnp.zeros_like(acc_dkvc)
-    pl.semaphore_wait(barrier, n_blk - 1)
+    pl.semaphore_wait(barrier, len(partners))
     cross_summary(0)
 
+    features_load.wait()
+
     def first(sl):
-        s = features[0, sl, :].T
+        s = out[0, sl, :].T
         stream[:, sl] = s
         cross_query(0, s, sl)
         place = coords[0, :, sl]
@@ -610,6 +885,9 @@
                 gates[l, e : e + 1, sl] = grown[e] / total
 
     each_tile(first)
+    cut_experts()
+    for ref in (g_up, g_down):
+        ref[...] = jnp.zeros_like(ref)
     cross_summary(1)
     cross_total(0)
     each_tile(lambda sl: cross_read(0, stream[:, sl], sl))
@@ -629,55 +907,111 @@
     acc_kv[...] = jnp.zeros_like(acc_kv)
     self_total(1)
 
+    cot_load.wait()
+
     def third(sl):
         s, y = self_read(1, stream[:, sl], sl)
-        ds = cot[0, sl, :].T
-        more, ds = experts_back(1, ds, y, sl, True)
+        ds = fgrad[0, sl, :].T
+        more, ds = experts_both(1, ds, y, sl)
         out[0, sl, :] = (s + more).T
         self_read_back(1, ds, sl)
         stream[:, sl] = ds
 
     each_tile(third)
     send_self_back(1)
+    reduce_pair(1, 0)
+    reduce_pair(1, 1)
+    tick()
     acc_kv[...] = jnp.zeros_like(acc_kv)
     self_total_back(1)
+    tick()
 
     def fourth(sl):
         ds = attention_back(1, stream[:, sl], sl)
-        _, ds = experts_back(0, ds, get(y_ref, 2, sl), sl, False)
+        dz = cross_read_back(1, ds, sl)
+        stream[:, sl] = cross_query_back(1, ds, dz, sl)
+
+    each_tile(fourth, ticks=(1,))
+    tick()
+
+    for pair in range(experts // 2):
+
+        def experts_of(sl, pair=pair):
+            ds2 = split(stream[:, sl])
+            y = get(y_ref, 2, sl)
+            dy = None
+            for e in (2 * pair, 2 * pair + 1):
+                _, part = expert_back(0, e, y, ds2, sl)
+                dy = part if dy is None else dy + part
+            dy_ref[:, sl] = dy if pair == 0 else dy_ref[:, sl] + dy
+
+        each_tile(experts_of, ticks=(1,))
+        reduce_pair(0, pair)
+        tick()
+
+    def fifth(sl):
+        ds = gates_back(0, stream[:, sl], dy_ref[:, sl], sl)
         self_read_back(0, ds, sl)
         stream[:, sl] = ds
 
-    each_tile(fourth)
+    each_tile(fifth)
     send_self_back(0)
     send_cross_back(1)
+    tick()
     acc_dkvc[...] = jnp.zeros_like(acc_dkvc)
+    for j in range(3):
+        finish_in(1, 1, j)
+    finish_out(1, 1)
+    finish_out(1, 0)
+    reduce_att(1, 1)
+    finish_in(1, 0, 0)
+    tick()
+    cross_keys_back(1)
+    finish_in(1, 0, 1)
+    finish_in(1, 0, 2)
+    reduce_att(1, 0)
     self_total_back(0)
-
-    def fifth(sl):
-        fgrad[0, sl, :] = attention_back(0, stream[:, sl], sl).T
-
-    each_tile(fifth)
+    tick()
+
+    def sixth(sl):
+        ds = attention_back(0, stream[:, sl], sl)
+        stream[:, sl] = ds
+        dy_ref[:, sl] = cross_read_back(0, ds, sl)
+
+    each_tile(sixth, ticks=(1,))
     send_cross_back(0)
-    cross_keys_back(1)
+    tick()
+    for j in range(3):
+        finish_in(0, 1, j)
+    finish_out(0, 1)
+    reduce_att(0, 1)
+    tick()
+
+    def seventh(sl):
+        fgrad[0, sl, :] = cross_query_back(0, stream[:, sl], dy_ref[:, sl], sl).T
+
+    each_tile(seventh)
+    tick()
+    finish_out(0, 0)
+    finish_in(0, 0, 0)
     cross_keys_back(0)
-
-    exact = functools.partial(
-        lax.dot_general, precision=lax.Precision.HIGHEST, preferred_element_type=F32
-    )
+    finish_in(0, 0, 1)
+    finish_in(0, 0, 2)
+    reduce_att(0, 0)
+    g_small[...] = jnp.zeros_like(g_small)
+    for at in range(layers * 3):
+        g_small[at : at + 1, :] = jnp.sum(acc_g[at].T, axis=0, keepdims=True)
     for l in range(layers):
-        for a in range(2):
-            for j in range(3):
-                at = a * 3 + j
-                g_in[l, a, j] = exact(
-                    acc_wi[l, at * d : (at + 1) * d, :], perm, (((0,), (0,)), ((), ()))
-                )
-            g_out[l, a] = exact(perm, acc_wo[l, a], (((0,), (0,)), ((), ())))
-        for j in range(3):
-            g_gain[l, j : j + 1, :] = jnp.sum(acc_g[l * 3 + j].T, axis=0, keepdims=True)
+        at = 8 * (l + 1)
+        g_small[at : at + 8, :] = acc_r[l]
+    if summed:
+        running.append(exchange_small(g_small, f_small, *ring[10:13]))
+    while running:
+        tick()
 
 
 def on_device(
+    n_dp,
     n_blk,
     features,
     func_points,
@@ -693,14 +1027,24 @@
     cotangent,
 ):
     layers, experts, d, hid = expert_up.shape
+    pairs = layers * 2
+    summed = n_dp % 2 == 0 and n_blk % 2 == 0 and (2 * d) % (8 * n_dp * n_blk) == 0
     count = features.shape[1]
     funcs, points = func_points.shape[1], func_points.shape[2]
     wide_hid = experts * hid
     shape = jax.ShapeDtypeStruct
     vmem = pl.BlockSpec(memory_space=pltpu.VMEM)
     smem = pl.BlockSpec(memory_space=pltpu.SMEM)
+    far = pl.BlockSpec(memory_space=pl.ANY)
     pair = pltpu.VMEM((layers, 2 * d, count), BF16)
+    up_shape, row_shape = (2 * d, hid), (4 * d, d)
     scratch = [
+        pltpu.VMEM(func_points.shape, F32),
+        pltpu.SemaphoreType.DMA((4 * layers + 5,)),
+        pltpu.VMEM(((pairs,) + row_shape) if summed else (8, 128), F32),
+        pltpu.VMEM(((pairs,) + up_shape) if summed else (8, 128), F32),
+        pltpu.VMEM(((pairs,) + row_shape) if summed else (8, 128), F32),
+        pltpu.VMEM((32, 128), F32),
         pltpu.VMEM((layers, 6 * d, 3 * d), BF16),
         pltpu.VMEM((layers, d, 3 * d), BF16),
         pltpu.VMEM((layers, d, 6 * d), BF16),
@@ -739,25 +1083,43 @@
         pltpu.VMEM((layers, 6 * d, d), F32),
         pltpu.VMEM((layers, 2, d, d), F32),
         pltpu.VMEM((layers * 3, d, 128), F32),
+        pltpu.VMEM((layers, 2 * experts, 128), F32),
+        pltpu.VMEM((d, count), F32),
+        pltpu.VMEM((experts, count), F32),
         pltpu.VMEM((2 * layers, funcs * MSG, d), F32),
         pltpu.VMEM((2 * layers, n_blk - 1, funcs * MSG, d), F32),
         pltpu.VMEM((2 * layers, MSG, d), F32),
         pltpu.VMEM((2 * layers, n_blk - 1, MSG, d), F32),
     ] + [pltpu.SemaphoreType.DMA((2 * layers, n_blk - 1))] * 4
+    if summed:
+        n_flat, n_line = n_dp, n_blk // 2
+        moves = 2 + 2 * (n_flat - 1) + 2 * (n_line - 1)
+        for segs, (high, width) in ((pairs, up_shape), (2 * pairs, row_shape)):
+            scratch += [
+                pltpu.VMEM((segs, high // 2, width), F32),
+                pltpu.VMEM((segs, n_flat - 1, high // 2 // n_flat, width), F32),
+                pltpu.VMEM((segs, n_line - 1, high // 2 // n_flat // n_line, width), F32),
+                pltpu.SemaphoreType.DMA((segs, moves)),
+                pltpu.SemaphoreType.DMA((segs, moves)),
+            ]
+        few = n_flat + n_line - 1
+        scratch += [
+            pltpu.VMEM((2 + n_flat + n_line, 32, 128), F32),
+            pltpu.SemaphoreType.DMA((few,)),
+            pltpu.SemaphoreType.DMA((few,)),
+        ]
     results = pl.pallas_call(
-        functools.partial(device_kernel, n_blk),
+        functools.partial(device_kernel, n_dp, n_blk, summed),
         out_shape=[
             shape(features.shape, F32),
             shape(features.shape, F32),
-            shape(norm_gain.shape, F32),
-            shape(in_proj.shape, F32),
-            shape(out_proj.shape, F32),
-            shape((layers, 2 * experts, 128), F32),
-            shape(expert_up.shape, F32),
-            shape(expert_down.shape, F32),
+            shape((pairs,) + row_shape, F32),
+            shape((pairs,) + up_shape, F32),
+            shape((pairs,) + row_shape, F32),
+            shape((32, 128), F32),
         ],
-        in_specs=[vmem, vmem, vmem, smem, smem, vmem, vmem, vmem, smem, vmem, vmem, vmem],
-        out_specs=[vmem] * 8,
+        in_specs=[far, far, vmem, smem, smem, vmem, far, far, smem, far, far, far],
+        out_specs=[vmem] * 6,
         scratch_shapes=scratch,
         compiler_params=pltpu.CompilerParams(
             collective_id=0, has_side_effects=True, vmem_limit_bytes=62 * 2**20
@@ -770,16 +1132,28 @@
         presence,
         valid_rows,
         norm_gain,
-        in_proj,
-        out_proj,
+        in_proj.reshape(pairs, 3 * d, d),
+        out_proj.reshape(pairs, d, d),
         router,
-        expert_up,
-        expert_down,
+        expert_up.reshape((pairs,) + up_shape),
+        expert_down.reshape((pairs,) + row_shape),
         cotangent,
     )
-    y, dx, gain_g, in_g, out_g, route_g, up_g, down_g = results
-    route_g = jnp.sum(route_g, axis=-1).reshape(router.shape)
-    return (y, dx) + lax.psum((gain_g, in_g, out_g, route_g, up_g, down_g), ("dp", "blk"))
+    y, dx, *grads = results
+    if not summed:
+        grads = lax.psum(grads, ("dp", "blk"))
+    att_g, up_g, down_g, small = grads
+    att_g = att_g.reshape(layers, 2, 4, d, d)
+    return (
+        y,
+        dx,
+        small[: layers * 3].reshape(norm_gain.shape),
+        att_g[:, :, :3],
+        att_g[:, :, 3],
+        jnp.sum(small[8 : 8 * (layers + 1)], axis=-1).reshape(router.shape),
+        up_g.reshape(expert_up.shape),
+        down_g.reshape(expert_down.shape),
+    )
 
 
 def solution(mesh):
@@ -798,7 +1172,7 @@
         P("dp", "blk", None),
     )
     return jax.shard_map(
-        functools.partial(on_device, mesh.shape["blk"]),
+        functools.partial(on_device, mesh.shape["dp"], mesh.shape["blk"]),
         mesh=mesh,
         in_specs=placed,
         out_specs=(P("dp", "blk", None), P("dp", "blk", None), P(), P(), P(), P(), P(), P()),

time: 286 us -> 177 us (0.62); the launches traced: 286 us -> 174 us
  waiting for transfers between devices: 97.2 us -> 0 us
  blocking collectives: 40.4 us -> 0 us
  Pallas kernels: 123 us -> 159 us
  between operations: 14.1 us -> 0.95 us
    psum x1 -> x0, waiting for transfers between devices: 97.1 us -> none  [on_device(): lax.psum((gain_g, in_g, out_g, route_g, up_g, down_g), ('dp', 'blk'))]
    psum x1 -> x0, blocking collectives: 40.4 us -> none  [on_device(): lax.psum((gain_g, in_g, out_g, route_g, up_g, down_g), ('dp', 'blk'))]
    pallas_call x1, Pallas kernels: 123 us -> 159 us  [on_device(): pl.pallas_call(functools.partial(device_kernel, n_dp, n_blk, summed), out...]
    unnamed x27 -> x21, local copies, waits for them, and re-layouts: 11.2 us -> 8.91 us
  transfers between devices with their start and end apart: 1 -> 0, of which waited for: 1 -> 0; matrix products, arithmetic and copies ran while one was open for 0% -> 0% of each run, Pallas kernels for 0% -> 0%
where the time goes in v2:
time: 177 us; the launch traced here: 174 us
  Pallas kernels  159 us (90%)
  local copies, waits for them, and re-layouts  13.4 us (8%)
    pallas_call x1, Pallas kernels, on_device(): pl.pallas_call(functools.partial(device_kernel, n_dp, n_blk, summed), out...  159 us
    unnamed x21, local copies, waits for them, and re-layouts  8.91 us

profile of v2, /device:TPU:0, one launch (start us, length us, event | category | flops | bytes accessed | tf_op | source)
XLA Modules:
  0.0 173.6 jit_solution(9307021324393397884)
XLA Ops:
  0.6 0.0 copy-start.6
  0.6 0.0 copy-start.5
  0.7 0.7 copy-done.6
  1.3 0.6 copy.24.valid
  1.9 0.0 copy-done.5
  1.9 0.6 copy.25.gain
  2.5 159.1 %gnot.1 = (f32[1,2048,128]{2,1,0:T(8,128)}, f32[1,2048,128]{2,1,0:T(8,128)}, f32[4,512,128]{2,1,0:T(8,128)}, f32[4,256,256]{2,1,0:T(8,128)}, f32[4,512,128]{2,1,0:T(8,128)}, /*index=5*/f32[32,128]{1,0:T(8,128)}) custom-call(f32[1,2048,128]{2,1,0:T(8,128)} %features_hbm.1, f32[1,3,512,128]{3,2,1,0:T(8,128)} %points_hbm.1, f32[1,2,2048]{2,1,0:T(2,128)} %coords.1, ...), custom_call_target="tpu_custom_call" | custom-call | tf_op jit(solution)/shard_map/gnot/pallas_call | solution.py:1111
  161.6 0.0 copy-start.4
  161.6 0.7 copy-done.4
  162.3 0.1 slice_reduce_fusion
  162.5 0.6 copy.27
  163.0 0.7 reshape.49
  163.7 0.0 copy-start.3
  163.7 1.8 %slice_bitcast_fusion = f32[2,2,128,128]{3,2,1,0:T(8,128)} fusion(f32[2,2,4,128,128]{4,3,2,1,0:T(8,128)} %bitcast.11), kind=kLoop, calls=%fused_computation | loop fusion | bytes 524288 | tf_op jit(solution)/shard_map/squeeze | solution.py:1152
  165.5 2.1 %slice.16 = f32[2,2,3,128,128]{4,3,2,1,0:T(8,128)} slice(f32[2,2,4,128,128]{4,3,2,1,0:T(8,128)} %bitcast.12), slice={[0:2], [0:2], [0:3], [0:128], [0:128]} | slice | bytes 1572864 | tf_op jit(solution)/shard_map/slice | solution.py:1151
  167.5 0.0 copy-done.3
  167.5 0.0 copy-start.2
  167.5 1.0 copy.33
  168.5 0.6 copy-done.2
  169.1 0.0 copy-start.1
  169.1 1.0 copy.34
  170.1 0.6 copy-done.1
  170.7 0.0 copy-start
  170.7 1.0 copy.35
  171.7 0.6 copy-done
  172.3 1.0 copy.36
  (2 shorter events, 0.0 us)
Async XLA Ops:
  0.6 0.7 copy-start.6
  0.6 1.3 copy-start.5
  161.6 0.7 copy-start.4
  163.7 3.8 %copy-start.3 = (f32[1,2048,128]{2,1,0:T(8,128)S(1)}, f32[1,2048,128]{2,1,0:T(8,128)}, u32[]{:S(2)}) copy-start(f32[1,2048,128]{2,1,0:T(8,128)} %get-tuple-element.44) | copy-start | bytes 3145732
  167.5 1.6 copy-start.2
  169.1 1.6 copy-start.1
  170.7 1.6 copy-start
